TPU v7x, 32 devices: a whole 2x2x4 slice. The times are simulated.
32 devices in a mesh: seq: 8 (over z, y), head: 4 (over x, core).
Axes of the slice: x: 2, y: 2, z: 4, core: 2. Of those that a mesh axis runs over, the one named last changes fastest.
Arguments:
- tokens: bfloat16 [3, 1024, 768], P(None, 'seq'), may hold values from -6 to 6
- cotangent: bfloat16 [3, 1024, 768], P(None, 'seq'), may hold values from -6 to 6
- lengths: int32 [3, 3], replicated, may hold values from 1 to 960, 1024 in all within a row
- coords: int32 [2, 3, 1024], P(None, None, 'seq'), may hold values from 0 to 255
- keep_mask: int32 [3, 1024], P(None, 'seq'), may hold values 0 or 1
- ln_gains: bfloat16 [2, 768], P(None, 'seq'), may hold values from 0.5 to 1.5
- ln_shifts: bfloat16 [2, 768], P(None, 'seq'), may hold values from -2 to 2
- out_bias: bfloat16 [2, 768], P(None, 'seq'), may hold values from -2 to 2
- w_qkv: bfloat16 [768, 3, 768], P('seq', None, 'head'), may hold values from -0.3125 to 0.3125
- qv_bias: bfloat16 [2, 768], P(None, 'head'), may hold values from -2 to 2
- w_out: bfloat16 [768, 768], P('head', 'seq'), may hold values from -1.75 to 1.75
- w_up: bfloat16 [768, 3072], P('seq', 'head'), may hold values from -0.21875 to 0.21875
- up_bias: bfloat16 [3072], P('head'), may hold values from -2 to 2
- w_down: bfloat16 [3072, 768], P('head', 'seq'), may hold values from -0.109375 to 0.109375
Outputs:
- out_tokens: bfloat16 [3, 1024, 768], P(None, 'seq')
- grad_tokens: bfloat16 [3, 1024, 768], P(None, 'seq')
- grad_ln_gains: float32 [2, 768], P(None, 'seq')
- grad_ln_shifts: float32 [2, 768], P(None, 'seq')
- grad_out_bias: float32 [2, 768], P(None, 'seq')
- grad_qkv: float32 [768, 3, 768], P('seq', None, 'head')
- grad_qv_bias: float32 [2, 768], P(None, 'head')
- grad_out: float32 [768, 768], P('head', 'seq')
- grad_up: float32 [768, 3072], P('seq', 'head')
- grad_up_bias: float32 [3072], P('head')
- grad_down: float32 [3072, 768], P('head', 'seq')
Inputs may be any that keep to these rules, and one draw needn't show every extreme that they name: Each micro-batch row holds 3 slides end to end, their lengths summing to 1024; the longest has exactly 960 tiles.
All inputs are finite; a program needn't handle non-finite values. No bound on the sum of `keep_mask` on one device may be relied on, other than what follows from the above.
Results may differ from a plain program's by a relative error of at most 0.02.
Values may be sent and summed in bfloat16 or wider, within the bound.
A program may use at most 256 MiB of HBM per device.

v0:
```python
from functools import partial
import math

import jax
import jax.numpy as jnp
from jax import lax
from jax.sharding import PartitionSpec as P

HDIM = 48
UNIT = 1024
BRANCHES = 5


EPSILON = 1e-05


def position_table(grid_rows, width):
    quarter = width // 4
    frequency = jnp.exp(-jnp.log(10000.0) * jnp.arange(quarter, dtype=jnp.float32) / quarter)
    along_row = grid_rows[0].astype(jnp.float32)[:, None] * frequency[None, :]
    along_col = grid_rows[1].astype(jnp.float32)[:, None] * frequency[None, :]
    return jnp.concatenate(
        [jnp.sin(along_row), jnp.cos(along_row), jnp.sin(along_col), jnp.cos(along_col)], axis=1
    )


def layer_norm(values, gain_vec, shift_vec):
    centre = values - jnp.mean(values, axis=-1, keepdims=True)
    spread = jnp.mean(centre * centre, axis=-1, keepdims=True)
    return centre * lax.rsqrt(spread + EPSILON) * gain_vec + shift_vec


def slide_of(positions, bounds):
    return jnp.sum((positions[:, None] >= bounds[None, :]).astype(jnp.int32), axis=1)


def pair_weight(query_pos, key_pos, key_keep, head_ids, bounds, seg_unit):
    same_slide = slide_of(query_pos, bounds)[:, None] == slide_of(key_pos, bounds)[None, :]
    visible = same_slide & ((key_keep[None, :] > 0) | (query_pos[:, None] == key_pos[None, :]))
    counted = jnp.zeros((head_ids.shape[0], query_pos.shape[0], key_pos.shape[0]), jnp.float32)
    for branch in range(BRANCHES):
        stride = 2**branch
        span = seg_unit * stride
        same_seg = query_pos[:, None] // span == key_pos[None, :] // span
        query_on = query_pos[None, :] % stride == head_ids[:, None] % stride
        key_on = key_pos[None, :] % stride == head_ids[:, None] % stride
        counted = counted + (same_seg[None] & query_on[:, :, None] & key_on[:, None, :]).astype(
            jnp.float32
        )
    return counted * visible[None].astype(jnp.float32)


def head_total(partial_sum):
    return lax.psum(partial_sum.astype(jnp.bfloat16), "head").astype(jnp.float32)


def per_device(
    tokens,
    cotangent,
    lengths,
    coords,
    keep_mask,
    ln_gains,
    ln_shifts,
    out_bias,
    w_qkv,
    qv_bias,
    w_out,
    w_up,
    up_bias,
    w_down,
):
    micro_count, tok_local, width = tokens.shape
    row_len = tok_local * lax.axis_size("seq")
    seg_unit = UNIT
    block_count = row_len // seg_unit
    heads_local = w_qkv.shape[2] // HDIM
    local_width = heads_local * HDIM
    inv_root = 1.0 / math.sqrt(HDIM)
    head_ids = lax.axis_index("head") * heads_local + jnp.arange(heads_local, dtype=jnp.int32)
    own_pos = lax.axis_index("seq") * tok_local + jnp.arange(tok_local, dtype=jnp.int32)
    block_starts = jnp.arange(block_count, dtype=jnp.int32) * seg_unit
    bias_qv = qv_bias.astype(jnp.float32)
    bias_up = up_bias.astype(jnp.float32)
    sum_qkv = jnp.zeros((width, 3, local_width), jnp.float32)
    sum_out = jnp.zeros((local_width, width), jnp.float32)
    sum_up = jnp.zeros((width, w_up.shape[1]), jnp.float32)
    sum_down = jnp.zeros((w_down.shape[0], width), jnp.float32)
    sum_gain = jnp.zeros((2, width), jnp.float32)
    sum_shift = jnp.zeros((2, width), jnp.float32)
    sum_obias = jnp.zeros((2, width), jnp.float32)
    sum_qvb = jnp.zeros((2, local_width), jnp.float32)
    sum_upb = jnp.zeros((w_up.shape[1],), jnp.float32)
    out_rows = []
    grad_rows = []
    for micro_id in range(micro_count):
        full_qkv, full_out, full_up, full_down, gain_rows, shift_rows, obias_rows = (
            lax.all_gather(w_qkv, "seq", axis=0, tiled=True),
            lax.all_gather(w_out, "seq", axis=1, tiled=True),
            lax.all_gather(w_up, "seq", axis=0, tiled=True),
            lax.all_gather(w_down, "seq", axis=1, tiled=True),
            lax.all_gather(ln_gains, "seq", axis=1, tiled=True),
            lax.all_gather(ln_shifts, "seq", axis=1, tiled=True),
            lax.all_gather(out_bias, "seq", axis=1, tiled=True),
        )
        gain_rows = gain_rows.astype(jnp.float32)
        shift_rows = shift_rows.astype(jnp.float32)
        obias_rows = obias_rows.astype(jnp.float32)
        bounds = jnp.cumsum(lengths[micro_id])[:-1]
        inputs = tokens[micro_id].astype(jnp.float32) + position_table(coords[:, micro_id], width)
        normed = layer_norm(inputs, gain_rows[0], shift_rows[0]).astype(jnp.bfloat16)
        projected = jnp.einsum("td,dcf->tcf", normed, full_qkv, preferred_element_type=jnp.float32)
        queries = (
            (projected[:, 0] + bias_qv[0])
            .astype(jnp.bfloat16)
            .reshape(tok_local, heads_local, HDIM)
        )
        key_rows = projected[:, 1].astype(jnp.bfloat16).reshape(tok_local, heads_local, HDIM)
        value_rows = (
            (projected[:, 2] + bias_qv[1])
            .astype(jnp.bfloat16)
            .reshape(tok_local, heads_local, HDIM)
        )
        keep_local = keep_mask[micro_id].astype(jnp.bfloat16)
        key_all, value_all, keep_all = (
            lax.all_gather(key_rows, "seq", axis=0, tiled=True),
            lax.all_gather(value_rows, "seq", axis=0, tiled=True),
            lax.all_gather(keep_local, "seq", axis=0, tiled=True),
        )

        def key_block(key_src, value_src, keep_src, offset):
            key_blk = lax.dynamic_slice_in_dim(key_src, offset, seg_unit, 0)
            value_blk = lax.dynamic_slice_in_dim(value_src, offset, seg_unit, 0)
            keep_blk = lax.dynamic_slice_in_dim(keep_src, offset, seg_unit, 0)
            key_pos = offset + jnp.arange(seg_unit, dtype=jnp.int32)
            scores = (
                jnp.einsum("thd,khd->htk", queries, key_blk, preferred_element_type=jnp.float32)
                * inv_root
            )
            weight = pair_weight(own_pos, key_pos, keep_blk, head_ids, bounds, seg_unit)
            return (key_blk, value_blk, scores, weight)

        def stats_step(running, offset):
            row_peak, row_total = running
            _, _, scores, weight = key_block(key_all, value_all, keep_all, offset)
            live = weight > 0
            new_peak = jnp.maximum(row_peak, jnp.max(jnp.where(live, scores, -1e30), axis=2))
            fresh = jnp.sum(
                jnp.where(live, weight * jnp.exp(scores - new_peak[:, :, None]), 0.0), axis=2
            )
            return ((new_peak, row_total * jnp.exp(row_peak - new_peak) + fresh), None)

        start_stats = (
            jnp.full((heads_local, tok_local), -1e30, jnp.float32),
            jnp.zeros((heads_local, tok_local), jnp.float32),
        )
        (row_peak, row_total), _ = lax.scan(stats_step, start_stats, block_starts)
        log_total = row_peak + jnp.log(row_total)

        def value_step(running, offset):
            _, value_blk, scores, weight = key_block(key_all, value_all, keep_all, offset)
            prob_low = (weight * jnp.exp(scores - log_total[:, :, None])).astype(jnp.bfloat16)
            return (
                running
                + jnp.einsum(
                    "htk,khd->thd", prob_low, value_blk, preferred_element_type=jnp.float32
                ),
                None,
            )

        attended, _ = lax.scan(
            value_step, jnp.zeros((tok_local, heads_local, HDIM), jnp.float32), block_starts
        )
        attended_low = attended.astype(jnp.bfloat16).reshape(tok_local, local_width)
        middle = (
            inputs
            + head_total(jnp.dot(attended_low, full_out, preferred_element_type=jnp.float32))
            + obias_rows[0]
        )
        normed_two = layer_norm(middle, gain_rows[1], shift_rows[1]).astype(jnp.bfloat16)
        hidden_pre = jnp.dot(normed_two, full_up, preferred_element_type=jnp.float32) + bias_up
        activated = jax.nn.gelu(hidden_pre, approximate=False).astype(jnp.bfloat16)
        result = (
            middle
            + head_total(jnp.dot(activated, full_down, preferred_element_type=jnp.float32))
            + obias_rows[1]
        )
        out_rows.append(result.astype(jnp.bfloat16))
        grad_out_low = cotangent[micro_id]
        grad_out_f32 = grad_out_low.astype(jnp.float32)
        sum_down = sum_down + jnp.einsum(
            "tf,td->fd", activated, grad_out_low, preferred_element_type=jnp.float32
        )
        grad_act = jnp.einsum(
            "td,fd->tf", grad_out_low, full_down, preferred_element_type=jnp.float32
        )
        _, gelu_back = jax.vjp(partial(jax.nn.gelu, approximate=False), hidden_pre)
        grad_pre_low = gelu_back(grad_act)[0].astype(jnp.bfloat16)
        sum_upb = sum_upb + jnp.sum(grad_pre_low.astype(jnp.float32), axis=0)
        sum_up = sum_up + jnp.einsum(
            "td,tf->df", normed_two, grad_pre_low, preferred_element_type=jnp.float32
        )
        grad_normed_two = head_total(
            jnp.einsum("tf,df->td", grad_pre_low, full_up, preferred_element_type=jnp.float32)
        )
        _, norm_back_two = jax.vjp(layer_norm, middle, gain_rows[1], shift_rows[1])
        grad_from_two, grad_gain_two, grad_shift_two = norm_back_two(grad_normed_two)
        grad_middle = grad_out_f32 + grad_from_two
        grad_branch_low = grad_middle.astype(jnp.bfloat16)
        sum_obias = sum_obias + jnp.stack(
            [jnp.sum(grad_branch_low.astype(jnp.float32), axis=0), jnp.sum(grad_out_f32, axis=0)]
        )
        sum_out = sum_out + jnp.einsum(
            "tf,td->fd", attended_low, grad_branch_low, preferred_element_type=jnp.float32
        )
        grad_attn_low = (
            jnp.einsum("td,fd->tf", grad_branch_low, full_out, preferred_element_type=jnp.float32)
            .astype(jnp.bfloat16)
            .reshape(tok_local, heads_local, HDIM)
        )
        row_delta = jnp.einsum("thd,thd->ht", grad_attn_low.astype(jnp.float32), attended)
        back_keys, back_values, back_keep = (
            lax.all_gather(key_rows, "seq", axis=0, tiled=True),
            lax.all_gather(value_rows, "seq", axis=0, tiled=True),
            lax.all_gather(keep_local, "seq", axis=0, tiled=True),
        )

        def key_side_step(running, offset):
            key_blk, value_blk, scores, weight = key_block(
                back_keys, back_values, back_keep, offset
            )
            prob_f32 = weight * jnp.exp(scores - log_total[:, :, None])
            grad_prob = jnp.einsum(
                "thd,khd->htk", grad_attn_low, value_blk, preferred_element_type=jnp.float32
            )
            grad_scores = (prob_f32 * (grad_prob - row_delta[:, :, None])).astype(jnp.bfloat16)
            running = running + jnp.einsum(
                "htk,khd->thd", grad_scores, key_blk, preferred_element_type=jnp.float32
            )
            prob_low = prob_f32.astype(jnp.bfloat16)
            key_term = (
                jnp.einsum("htk,thd->khd", grad_scores, queries, preferred_element_type=jnp.float32)
                * inv_root
            )
            value_term = jnp.einsum(
                "htk,thd->khd", prob_low, grad_attn_low, preferred_element_type=jnp.float32
            )
            return (
                running,
                jnp.concatenate(
                    [
                        key_term.reshape(seg_unit, local_width),
                        value_term.reshape(seg_unit, local_width),
                    ],
                    axis=1,
                ),
            )

        query_sum, terms = lax.scan(
            key_side_step, jnp.zeros((tok_local, heads_local, HDIM), jnp.float32), block_starts
        )
        owned = lax.psum_scatter(
            terms.reshape(row_len, 2 * local_width), "seq", scatter_dimension=0, tiled=True
        )
        grad_queries = query_sum * inv_root
        grad_keys = owned[:, :local_width].reshape(tok_local, heads_local, HDIM)
        grad_values = owned[:, local_width:].reshape(tok_local, heads_local, HDIM)
        grad_q_low = grad_queries.astype(jnp.bfloat16).reshape(tok_local, local_width)
        grad_k_low = grad_keys.astype(jnp.bfloat16).reshape(tok_local, local_width)
        grad_v_low = grad_values.astype(jnp.bfloat16).reshape(tok_local, local_width)
        sum_qvb = sum_qvb + jnp.stack(
            [
                jnp.sum(grad_q_low.astype(jnp.float32), axis=0),
                jnp.sum(grad_v_low.astype(jnp.float32), axis=0),
            ]
        )
        grad_proj = jnp.stack([grad_q_low, grad_k_low, grad_v_low], axis=1)
        sum_qkv = sum_qkv + jnp.einsum(
            "td,tcf->dcf", normed, grad_proj, preferred_element_type=jnp.float32
        )
        grad_normed = head_total(
            jnp.einsum("tcf,dcf->td", grad_proj, full_qkv, preferred_element_type=jnp.float32)
        )
        _, norm_back_one = jax.vjp(layer_norm, inputs, gain_rows[0], shift_rows[0])
        grad_from_one, grad_gain_one, grad_shift_one = norm_back_one(grad_normed)
        grad_rows.append((grad_middle + grad_from_one).astype(jnp.bfloat16))
        sum_gain = sum_gain + jnp.stack([grad_gain_one, grad_gain_two])
        sum_shift = sum_shift + jnp.stack([grad_shift_one, grad_shift_two])
    grad_qkv, grad_out, grad_up, grad_down, grad_gain, grad_shift, grad_obias = (
        lax.psum_scatter(sum_qkv, "seq", scatter_dimension=0, tiled=True),
        lax.psum_scatter(sum_out, "seq", scatter_dimension=1, tiled=True),
        lax.psum_scatter(sum_up, "seq", scatter_dimension=0, tiled=True),
        lax.psum_scatter(sum_down, "seq", scatter_dimension=1, tiled=True),
        lax.psum_scatter(sum_gain, "seq", scatter_dimension=1, tiled=True),
        lax.psum_scatter(sum_shift, "seq", scatter_dimension=1, tiled=True),
        lax.psum_scatter(sum_obias, "seq", scatter_dimension=1, tiled=True),
    )
    grad_qvb, grad_upb = lax.psum((sum_qvb, sum_upb), "seq")
    return (
        jnp.stack(out_rows),
        jnp.stack(grad_rows),
        grad_gain,
        grad_shift,
        grad_obias,
        grad_qkv,
        grad_qvb,
        grad_out,
        grad_up,
        grad_upb,
        grad_down,
    )


def solution(mesh):
    placed = (
        P(None, "seq", None),
        P(None, "seq", None),
        P(),
        P(None, None, "seq"),
        P(None, "seq"),
        P(None, "seq"),
        P(None, "seq"),
        P(None, "seq"),
        P("seq", None, "head"),
        P(None, "head"),
        P("head", "seq"),
        P("seq", "head"),
        P("head"),
        P("head", "seq"),
    )
    return jax.shard_map(
        per_device,
        mesh=mesh,
        in_specs=placed,
        out_specs=(
            P(None, "seq", None),
            P(None, "seq", None),
            P(None, "seq"),
            P(None, "seq"),
            P(None, "seq"),
            P("seq", None, "head"),
            P(None, "head"),
            P("head", "seq"),
            P("seq", "head"),
            P("head"),
            P("head", "seq"),
        ),
        check_vma=False,
    )
```

profile of v0, /device:TPU:0, one launch (start us, length us, event | category | flops | bytes accessed | tf_op | source)
XLA Modules:
  0.0 1200.9 jit_solution(1397354520429183418)
XLA Ops:
  16.9 22.3 %all-gather.3 = bf16[8,96,2]{1,2,0:T(2,128)(2,1)S(1)} all-gather(bf16[1,96,2]{1,2,0:T(2,128)(2,1)} %bitcast.359), channel_id=1, replica_groups=mesh['seq'=8,'head'=4] {'seq'}, dimensions={0}, use_global_device_ids=true | all-gather | bytes 3456 | tf_op jit(solution)/shard_map/all_gather | solution.py:102
  39.3 16.4 %all-gather.4 = bf16[8,96,2]{1,2,0:T(2,128)(2,1)S(1)} all-gather(bf16[1,96,2]{1,2,0:T(2,128)(2,1)} %bitcast.360), channel_id=1, replica_groups=mesh['seq'=8,'head'=4] {'seq'}, dimensions={0}, use_global_device_ids=true | all-gather | bytes 3456 | tf_op jit(solution)/shard_map/all_gather | solution.py:103
  56.8 35.8 %all_gather.34 = bf16[768,3,192]{2,1,0:T(4,128)(2,1)S(1)} all-gather(bf16[96,3,192]{2,1,0:T(4,128)(2,1)S(1)} %copy.72), channel_id=1, replica_groups=mesh['seq'=8,'head'=4] {'seq'}, dimensions={0}, use_global_device_ids=true | all-gather | bytes 995328 | tf_op jit(solution)/shard_map/all_gather | solution.py:98
  93.5 2.8 multiply_sine_fusion.5
  100.5 18.6 %all-gather.1 = bf16[1,1024]{1,0:T(2,128)(2,1)S(1)} all-gather(bf16[1,128]{1,0:T(2,128)(2,1)S(1)} %get-tuple-element.452), channel_id=3, replica_groups=mesh['seq'=8,'head'=4] {'seq'}, dimensions={1}, use_global_device_ids=true | all-gather | bytes 2304 | tf_op jit(solution)/shard_map/all_gather | solution.py:128
  119.2 16.2 %all-gather.2 = bf16[1,1024]{1,0:T(2,128)(2,1)S(1)} all-gather(bf16[1,128]{1,0:T(2,128)(2,1)S(1)} %get-tuple-element.453), channel_id=4, replica_groups=mesh['seq'=8,'head'=4] {'seq'}, dimensions={1}, use_global_device_ids=true | all-gather | bytes 2304 | tf_op jit(solution)/shard_map/all_gather | solution.py:128
  135.3 18.2 %all-gather = bf16[1,1024]{1,0:T(2,128)(2,1)S(1)} all-gather(bf16[1,128]{1,0:T(2,128)(2,1)S(1)} %get-tuple-element.454), channel_id=2, replica_groups=mesh['seq'=8,'head'=4] {'seq'}, dimensions={1}, use_global_device_ids=true | all-gather | bytes 2304 | tf_op jit(solution)/shard_map/all_gather | solution.py:128
  154.3 31.3 %all_gather.38 = bf16[192,768]{0,1:T(8,128)(2,1)S(1)} all-gather(bf16[192,96]{0,1:T(8,128)(2,1)S(1)} %copy.74), channel_id=1, replica_groups=mesh['seq'=8,'head'=4] {'seq'}, dimensions={1}, use_global_device_ids=true | all-gather | bytes 331776 | tf_op jit(solution)/shard_map/all_gather | solution.py:99
  185.7 27.1 %all_gather.37 = bf16[1024,4,48]{0,2,1:T(8,128)(2,1)S(1)} all-gather(bf16[128,4,48]{0,2,1:T(8,128)(2,1)S(1)} %bitcast.348), channel_id=1, replica_groups=mesh['seq'=8,'head'=4] {'seq'}, dimensions={0}, use_global_device_ids=true | all-gather | bytes 442368 | tf_op jit(solution)/shard_map/all_gather | solution.py:126
  212.8 26.7 %all_gather.35 = bf16[1024,4,48]{0,2,1:T(8,128)(2,1)S(1)} all-gather(bf16[128,4,48]{0,2,1:T(8,128)(2,1)S(1)} %get-tuple-element.434), channel_id=1, replica_groups=mesh['seq'=8,'head'=4] {'seq'}, dimensions={0}, use_global_device_ids=true | all-gather | bytes 442368 | tf_op jit(solution)/shard_map/all_gather | solution.py:127
  239.6 26.7 %all_gather.86 = bf16[1024,4,48]{0,2,1:T(8,128)(2,1)S(1)} all-gather(bf16[128,4,48]{0,2,1:T(8,128)(2,1)S(1)} %bitcast.347), channel_id=1, replica_groups=mesh['seq'=8,'head'=4] {'seq'}, dimensions={0}, use_global_device_ids=true | all-gather | bytes 442368 | tf_op jit(solution)/shard_map/all_gather | solution.py:126
  266.3 27.2 %all_gather.83 = bf16[1024,4,48]{0,2,1:T(8,128)(2,1)S(1)} all-gather(bf16[128,4,48]{0,2,1:T(8,128)(2,1)S(1)} %bitcast.346), channel_id=1, replica_groups=mesh['seq'=8,'head'=4] {'seq'}, dimensions={0}, use_global_device_ids=true | all-gather | bytes 442368 | tf_op jit(solution)/shard_map/all_gather | solution.py:126
  293.5 26.7 %all_gather.81 = bf16[1024,4,48]{0,2,1:T(8,128)(2,1)S(1)} all-gather(bf16[128,4,48]{0,2,1:T(8,128)(2,1)S(1)} %get-tuple-element.435), channel_id=1, replica_groups=mesh['seq'=8,'head'=4] {'seq'}, dimensions={0}, use_global_device_ids=true | all-gather | bytes 442368 | tf_op jit(solution)/shard_map/all_gather | solution.py:127
  320.2 27.2 %all_gather.84 = bf16[1024,4,48]{0,2,1:T(8,128)(2,1)S(1)} all-gather(bf16[128,4,48]{0,2,1:T(8,128)(2,1)S(1)} %get-tuple-element.436), channel_id=1, replica_groups=mesh['seq'=8,'head'=4] {'seq'}, dimensions={0}, use_global_device_ids=true | all-gather | bytes 442368 | tf_op jit(solution)/shard_map/all_gather | solution.py:127
  349.3 2.4 select_reduce_fusion.5
  351.7 2.8 select_reduce_fusion.4
  354.6 3.5 select_reduce_fusion.2
  358.1 2.7 exponential_multiply_fusion.1
  360.9 2.8 exponential_multiply_fusion.2
  372.4 16.2 %all-gather.5 = bf16[8,96,2]{1,2,0:T(2,128)(2,1)S(1)} all-gather(bf16[1,96,2]{1,2,0:T(2,128)(2,1)S(1)} %bitcast.361), channel_id=1, replica_groups=mesh['seq'=8,'head'=4] {'seq'}, dimensions={0}, use_global_device_ids=true | all-gather | bytes 3456 | tf_op jit(solution)/shard_map/all_gather | solution.py:104
  389.3 13.2 %all-reduce.12.cloned.1.call-done = (bf16[128,768]{1,0:T(8,128)(2,1)}, bf16[128,768]{1,0:T(8,128)(2,1)}, bf16[128,768]{1,0:T(8,128)(2,1)}) async-done(((bf16[128,768]{1,0:T(8,128)(2,1)}, bf16[128,768]{1,0:T(8,128)(2,1)}, bf16[128,768]{1,0:T(8,128)(2,1)}), (bf16[128,768]{1,0:T(8,128)(2,1)}, bf16[128,768]{1,0:T(8,128)(2,1)}, bf16[128,768]{1,0:T(8,128)(2,1)})) %all-reduce.12.cloned.1.call-update) | async-done | bytes 589840 | tf_op jit(solution)/shard_map/psum | solution.py:54
  405.4 7.0 all-gather.9.cloned.1.call-done
  412.4 2.5 convolution_add_fusion.2
  414.9 39.6 %all-gather.11.cloned.1.call-done = bf16[768,768]{0,1:T(8,128)(2,1)} async-done(((bf16[768,96]{0,1:T(8,128)(2,1)}), bf16[768,768]{0,1:T(8,128)(2,1)}) %all-gather.11.cloned.1.call-update) | async-done | bytes 1179664 | tf_op jit(solution)/shard_map/all_gather | solution.py:101
  454.5 3.3 convert_reduce_fusion.9
  470.2 32.2 %all-reduce.10.cloned.1.call-done = (bf16[128,768]{1,0:T(8,128)(2,1)}, bf16[128,768]{1,0:T(8,128)(2,1)}, bf16[128,768]{1,0:T(8,128)(2,1)}) async-done(((bf16[128,768]{1,0:T(8,128)(2,1)}, bf16[128,768]{1,0:T(8,128)(2,1)}, bf16[128,768]{1,0:T(8,128)(2,1)}), (bf16[128,768]{1,0:T(8,128)(2,1)}, bf16[128,768]{1,0:T(8,128)(2,1)}, bf16[128,768]{1,0:T(8,128)(2,1)})) %all-reduce.10.cloned.1.call-update) | async-done | bytes 589840 | tf_op jit(solution)/shard_map/psum | solution.py:54
  502.4 2.6 fusion.48
  505.1 2.0 fusion.169
  524.5 2.6 convolution_convert_fusion.7
  527.1 2.6 convolution_convert_fusion.5
  529.7 2.0 fusion.164
  531.7 2.0 fusion.162
  539.0 40.6 %reduce-scatter.23.cloned.1.call-done = f32[128,384]{0,1:T(8,128)} async-done(((f32[1024,384]{0,1:T(8,128)}), f32[128,384]{0,1:T(8,128)}) %reduce-scatter.23.cloned.1.call-update) | async-done | bytes 196624 | tf_op jit(solution)/shard_map/reduce_scatter | solution.py:262
  580.5 67.4 %reduce-scatter.21.cloned.1.call-done = f32[128,384]{0,1:T(8,128)} async-done(((f32[1024,384]{0,1:T(8,128)}), f32[128,384]{0,1:T(8,128)}) %reduce-scatter.21.cloned.1.call-update) | async-done | bytes 196624 | tf_op jit(solution)/shard_map/reduce_scatter | solution.py:262
  649.0 66.9 %reduce-scatter.19.cloned.1.call-done = f32[128,384]{0,1:T(8,128)} async-done(((f32[1024,384]{0,1:T(8,128)}), f32[128,384]{0,1:T(8,128)}) %reduce-scatter.19.cloned.1.call-update) | async-done | bytes 196624 | tf_op jit(solution)/shard_map/reduce_scatter | solution.py:262
  722.8 34.8 %all-reduce.8.cloned.1.call-done = (bf16[128,768]{1,0:T(8,128)(2,1)}, bf16[128,768]{1,0:T(8,128)(2,1)}, bf16[128,768]{1,0:T(8,128)(2,1)}, bf16[128,768]{1,0:T(8,...) async-done(((bf16[128,768]{1,0:T(8,128)(2,1)}, bf16[128,768]{1,0:T(8,128)(2,1)}, bf16[128,768]{1,0:T(8,128)(2,1)}, bf16[128,768]{1,0:T(8,128)(2,1)}, ...) | async-done | bytes 1179664 | tf_op jit(solution)/shard_map/psum | solution.py:54
  759.0 2.3 convert_reduce_fusion.4
  761.4 2.4 convert_reduce_fusion.6
  767.1 4.4 add_add_fusion.1
  773.4 2.8 add_add_fusion
  778.5 2.1 add_add_fusion.2
  789.6 22.4 %all-reduce = (f32[2,192]{1,0:T(2,128)}, f32[768]{0:T(1024)}) all-reduce(f32[2,192]{1,0:T(2,128)S(1)} %fusion.141, f32[768]{0:T(1024)} %add_add_fusion.12), channel_id=1, replica_groups=mesh['seq'=8,'head'=4] {'seq'}, use_global_device_ids=true, to_apply=%region_82.83 | all-reduce | flops 1152 | bytes 9216 | tf_op jit(solution)/shard_map/psum | solution.py:298
  817.8 31.9 %reduce-scatter.31.cloned.1.call-done = f32[96,2]{1,0:T(8,128)} async-done(((f32[768,2]{1,0:T(8,128)}), f32[96,2]{1,0:T(8,128)}) %reduce-scatter.31.cloned.1.call-update) | async-done | bytes 784
  851.2 62.2 %reduce-scatter.35.cloned.1.call-done = f32[96,2]{1,0:T(8,128)} async-done(((f32[768,2]{1,0:T(8,128)}), f32[96,2]{1,0:T(8,128)}) %reduce-scatter.35.cloned.1.call-update) | async-done | bytes 784
  914.8 62.3 %reduce-scatter.33.cloned.1.call-done = f32[96,2]{1,0:T(8,128)} async-done(((f32[768,2]{1,0:T(8,128)}), f32[96,2]{1,0:T(8,128)}) %reduce-scatter.33.cloned.1.call-update) | async-done | bytes 784
  978.5 70.6 %reduce-scatter.27.cloned.1.call-done = f32[96,768]{1,0:T(8,128)} async-done(((f32[768,768]{1,0:T(8,128)}), f32[96,768]{1,0:T(8,128)}) %reduce-scatter.27.cloned.1.call-update) | async-done | bytes 294928 | tf_op jit(solution)/shard_map/reduce_scatter | solution.py:292
  1049.1 72.0 %reduce-scatter.29.cloned.1.call-done = f32[768,96]{0,1:T(8,128)} async-done(((f32[768,768]{0,1:T(8,128)}), f32[768,96]{0,1:T(8,128)}) %reduce-scatter.29.cloned.1.call-update) | async-done | bytes 294928 | tf_op jit(solution)/shard_map/reduce_scatter | solution.py:293
  1121.1 72.2 %reduce-scatter.25.cloned.1.call-done = f32[96,3,192]{2,0,1:T(8,128)} async-done(((f32[768,3,192]{2,0,1:T(8,128)}), f32[96,3,192]{2,0,1:T(8,128)}) %reduce-scatter.25.cloned.1.call-update) | async-done | bytes 221200 | tf_op jit(solution)/shard_map/reduce_scatter | solution.py:290
  (593 shorter events, 100.2 us)
Async XLA Ops:
  8.0 394.4 %all-reduce.12.cloned.1.call-start = ((), (), s32[]{:S(2)}) async-start(), calls=%async_computation.24 | async-start | bytes 1179648 | tf_op jit(solution)/shard_map/psum | solution.py:54
  97.7 254.0 %copy-start.96 = (f32[128,1,192]{0,2,1:T(8,128)}, f32[128,1,192]{0,2,1:T(8,128)S(1)}, u32[]{:S(2)}) copy-start(f32[128,1,192]{0,2,1:T(8,128)S(1)} %get-tuple-element.394) | copy-start | bytes 294916
  97.9 56.3 %copy-start.102 = (bf16[192,96]{1,0:T(8,128)(2,1)S(1)}, bf16[192,96]{1,0:T(8,128)(2,1)}, u32[]{:S(2)}) copy-start(bf16[192,96]{1,0:T(8,128)(2,1)} %param.24) | copy-start | bytes 110596
  99.2 248.2 %copy-start.126 = (s32[1024]{0:T(1024)S(1)}, s32[1024]{0:T(1024)}, u32[]{:S(2)}) copy-start(s32[1024]{0:T(1024)} %add_select_fusion.1) | copy-start | bytes 12292
  99.2 248.2 %copy-start.167 = (s32[128]{0:T(128)S(1)}, s32[128]{0:T(128)}, u32[]{:S(2)}) copy-start(s32[128]{0:T(128)} %get-tuple-element.497) | copy-start | bytes 1540
  99.3 248.3 %copy-start.125 = (s32[1024]{0:T(1024)S(1)}, s32[1024]{0:T(1024)}, u32[]{:S(2)}) copy-start(s32[1024]{0:T(1024)} %add_select_fusion.3) | copy-start | bytes 12292
  99.3 248.3 %copy-start.168 = (s32[128]{0:T(128)S(1)}, s32[128]{0:T(128)}, u32[]{:S(2)}) copy-start(s32[128]{0:T(128)} %get-tuple-element.499) | copy-start | bytes 1540
  99.3 249.9 %copy-start.94 = (f32[128,1,192]{0,2,1:T(8,128)}, f32[128,1,192]{0,2,1:T(8,128)S(1)}, u32[]{:S(2)}) copy-start(f32[128,1,192]{0,2,1:T(8,128)S(1)} %get-tuple-element.392) | copy-start | bytes 294916
  99.3 248.4 %copy-start.124 = (s32[1024]{0:T(1024)S(1)}, s32[1024]{0:T(1024)}, u32[]{:S(2)}) copy-start(s32[1024]{0:T(1024)} %add_select_fusion.5) | copy-start | bytes 12292
  99.3 248.4 %copy-start.165 = (s32[128]{0:T(128)S(1)}, s32[128]{0:T(128)}, u32[]{:S(2)}) copy-start(s32[128]{0:T(128)} %get-tuple-element.501) | copy-start | bytes 1540
  100.1 247.8 %copy-start.123 = (s32[1024]{0:T(1024)S(1)}, s32[1024]{0:T(1024)}, u32[]{:S(2)}) copy-start(s32[1024]{0:T(1024)} %add_select_fusion.7) | copy-start | bytes 12292
  100.1 247.8 %copy-start.166 = (s32[128]{0:T(128)S(1)}, s32[128]{0:T(128)}, u32[]{:S(2)}) copy-start(s32[128]{0:T(128)} %get-tuple-element.503) | copy-start | bytes 1540
  100.5 251.2 %copy-start.100 = (f32[4,48]{1,0:T(4,128)}, f32[4,48]{1,0:T(4,128)S(1)}, u32[]{:S(2)}) copy-start(f32[4,48]{1,0:T(4,128)S(1)} %add.1351) | copy-start | bytes 2308
  153.6 200.9 %copy-start.140 = (pred[4,128]{1,0:T(4,128)(4,1)}, pred[4,128]{1,0:T(4,128)(4,1)S(1)}, u32[]{:S(2)}) copy-start(pred[4,128]{1,0:T(4,128)(4,1)S(1)} %broadcast_compare_fusion.11) | copy-start | bytes 1540
  153.8 200.7 %copy-start.142 = (pred[4,128]{1,0:T(4,128)(4,1)}, pred[4,128]{1,0:T(4,128)(4,1)S(1)}, u32[]{:S(2)}) copy-start(pred[4,128]{1,0:T(4,128)(4,1)S(1)} %broadcast_compare_fusion.10) | copy-start | bytes 1540
  153.9 200.6 %copy-start.144 = (pred[4,128]{1,0:T(4,128)(4,1)}, pred[4,128]{1,0:T(4,128)(4,1)S(1)}, u32[]{:S(2)}) copy-start(pred[4,128]{1,0:T(4,128)(4,1)S(1)} %broadcast_compare_fusion.9) | copy-start | bytes 1540
  154.1 200.4 %copy-start.146 = (pred[4,128]{1,0:T(4,128)(4,1)}, pred[4,128]{1,0:T(4,128)(4,1)S(1)}, u32[]{:S(2)}) copy-start(pred[4,128]{1,0:T(4,128)(4,1)S(1)} %broadcast_compare_fusion.8) | copy-start | bytes 1540
  154.2 193.9 %copy-start.122 = (s32[1024]{0:T(1024)S(1)}, s32[1024]{0:T(1024)}, u32[]{:S(2)}) copy-start(s32[1024]{0:T(1024)} %add_select_fusion.8) | copy-start | bytes 12292
  154.2 193.9 %copy-start.164 = (s32[128]{0:T(128)S(1)}, s32[128]{0:T(128)}, u32[]{:S(2)}) copy-start(s32[128]{0:T(128)} %and_select_fusion.12) | copy-start | bytes 1540
  185.7 183.9 %copy-start.10 = (bf16[192,768]{0,1:T(8,128)(2,1)}, bf16[192,768]{0,1:T(8,128)(2,1)S(1)}, u32[]{:S(2)}) copy-start(bf16[192,768]{0,1:T(8,128)(2,1)S(1)} %all_gather.38) | copy-start | bytes 884740
  212.7 136.5 %copy-start.48 = (bf16[1024,4,48]{0,2,1:T(8,128)(2,1)}, bf16[1024,4,48]{0,2,1:T(8,128)(2,1)S(1)}, u32[]{:S(2)}) copy-start(bf16[1024,4,48]{0,2,1:T(8,128)(2,1)S(1)} %all_gather.37) | copy-start | bytes 1179652
  239.6 128.8 %copy-start.34 = (bf16[1024,4,48]{0,2,1:T(8,128)(2,1)}, bf16[1024,4,48]{0,2,1:T(8,128)(2,1)S(1)}, u32[]{:S(2)}) copy-start(bf16[1024,4,48]{0,2,1:T(8,128)(2,1)S(1)} %all_gather.35) | copy-start | bytes 1179652
  266.3 82.4 %copy-start.40 = (bf16[1024,4,48]{0,2,1:T(8,128)(2,1)}, bf16[1024,4,48]{0,2,1:T(8,128)(2,1)S(1)}, u32[]{:S(2)}) copy-start(bf16[1024,4,48]{0,2,1:T(8,128)(2,1)S(1)} %all_gather.86) | copy-start | bytes 1179652
  293.5 58.2 %copy-start.50 = (bf16[1024,4,48]{0,2,1:T(8,128)(2,1)}, bf16[1024,4,48]{0,2,1:T(8,128)(2,1)S(1)}, u32[]{:S(2)}) copy-start(bf16[1024,4,48]{0,2,1:T(8,128)(2,1)S(1)} %all_gather.83) | copy-start | bytes 1179652
  371.1 41.3 %all-gather.9.cloned.1.call-start = ((), (), s32[]{:S(2)}) async-start(), calls=%async_computation.10 | async-start | bytes 1327104 | tf_op jit(solution)/shard_map/all_gather | solution.py:100
  371.7 82.8 %all-gather.11.cloned.1.call-start = ((), (), s32[]{:S(2)}) async-start(), calls=%async_computation.11 | async-start | bytes 1327104 | tf_op jit(solution)/shard_map/all_gather | solution.py:101
  372.3 130.1 %all-reduce.10.cloned.1.call-start = ((), (), s32[]{:S(2)}) async-start(), calls=%async_computation.23 | async-start | bytes 1179648 | tf_op jit(solution)/shard_map/psum | solution.py:54
  404.0 101.0 %copy-start.128 = (f32[128]{0:T(128)}, f32[128]{0:T(128)S(1)}, u32[]{:S(2)}) copy-start(f32[128]{0:T(128)S(1)} %broadcast_multiply_fusion) | copy-start | bytes 1540
  405.4 99.7 %copy-start.136 = (f32[128]{0:T(128)}, f32[128]{0:T(128)S(1)}, u32[]{:S(2)}) copy-start(f32[128]{0:T(128)S(1)} %fusion.151) | copy-start | bytes 1540
  469.9 109.7 %reduce-scatter.23.cloned.1.call-start = ((), (), s32[]{:S(2)}) async-start(), calls=%async_computation.14 | async-start | bytes 1769472 | tf_op jit(solution)/shard_map/reduce_scatter | solution.py:262
  513.7 134.3 %reduce-scatter.21.cloned.1.call-start = ((), (), s32[]{:S(2)}) async-start(), calls=%async_computation.13 | async-start | bytes 1769472 | tf_op jit(solution)/shard_map/reduce_scatter | solution.py:262
  519.1 196.8 %reduce-scatter.19.cloned.1.call-start = ((), (), s32[]{:S(2)}) async-start(), calls=%async_computation.12 | async-start | bytes 1769472 | tf_op jit(solution)/shard_map/reduce_scatter | solution.py:262
  524.5 233.0 %all-reduce.8.cloned.1.call-start = ((), (), s32[]{:S(2)}) async-start(), calls=%async_computation.22 | async-start | bytes 2359296 | tf_op jit(solution)/shard_map/psum | solution.py:54
  536.7 180.2 %copy-start.67 = (bf16[4,48,128]{2,1,0:T(8,128)(2,1)}, bf16[4,48,128]{2,1,0:T(8,128)(2,1)S(1)}, u32[]{:S(2)}) copy-start(bf16[4,48,128]{2,1,0:T(8,128)(2,1)S(1)} %get-tuple-element.485) | copy-start | bytes 147460
  537.8 180.1 %copy-start.73 = (bf16[4,48,128]{2,1,0:T(8,128)(2,1)}, bf16[4,48,128]{2,1,0:T(8,128)(2,1)S(1)}, u32[]{:S(2)}) copy-start(bf16[4,48,128]{2,1,0:T(8,128)(2,1)S(1)} %get-tuple-element.483) | copy-start | bytes 147460
  539.0 181.2 %copy-start.75 = (bf16[4,48,128]{2,1,0:T(8,128)(2,1)}, bf16[4,48,128]{2,1,0:T(8,128)(2,1)S(1)}, u32[]{:S(2)}) copy-start(bf16[4,48,128]{2,1,0:T(8,128)(2,1)S(1)} %get-tuple-element.481) | copy-start | bytes 147460
  648.9 69.1 %copy-start.63 = (bf16[128,384]{0,1:T(8,128)(2,1)}, bf16[128,384]{0,1:T(8,128)(2,1)S(1)}, u32[]{:S(2)}) copy-start(bf16[128,384]{0,1:T(8,128)(2,1)S(1)} %convert.34) | copy-start | bytes 294916
  648.9 68.0 %copy-start.69 = (bf16[128,1,192]{0,2,1:T(8,128)(2,1)}, bf16[128,1,192]{0,2,1:T(8,128)(2,1)S(1)}, u32[]{:S(2)}) copy-start(bf16[128,1,192]{0,2,1:T(8,128)(2,1)S(1)} %get-tuple-element.401) | copy-start | bytes 147460
  648.9 68.0 %copy-start.71 = (bf16[128,1,192]{0,2,1:T(8,128)(2,1)}, bf16[128,1,192]{0,2,1:T(8,128)(2,1)S(1)}, u32[]{:S(2)}) copy-start(bf16[128,1,192]{0,2,1:T(8,128)(2,1)S(1)} %get-tuple-element.402) | copy-start | bytes 147460
  648.9 70.2 %copy-start.81 = (bf16[128,1,192]{0,2,1:T(8,128)(2,1)}, bf16[128,1,192]{0,2,1:T(8,128)(2,1)S(1)}, u32[]{:S(2)}) copy-start(bf16[128,1,192]{0,2,1:T(8,128)(2,1)S(1)} %get-tuple-element.399) | copy-start | bytes 147460
  649.0 70.2 %copy-start.83 = (bf16[128,1,192]{0,2,1:T(8,128)(2,1)}, bf16[128,1,192]{0,2,1:T(8,128)(2,1)S(1)}, u32[]{:S(2)}) copy-start(bf16[128,1,192]{0,2,1:T(8,128)(2,1)S(1)} %get-tuple-element.400) | copy-start | bytes 147460
  720.2 65.9 %reduce-scatter.37.cloned.1.call-start = ((), (), s32[]{:S(2)}) async-start(), calls=%async_computation.21 | async-start | bytes 884736
  722.5 127.3 %reduce-scatter.31.cloned.1.call-start = ((), (), s32[]{:S(2)}) async-start(), calls=%async_computation.18 | async-start | bytes 442368
  764.8 148.6 %reduce-scatter.35.cloned.1.call-start = ((), (), s32[]{:S(2)}) async-start(), calls=%async_computation.20 | async-start | bytes 442368
  765.9 211.2 %reduce-scatter.33.cloned.1.call-start = ((), (), s32[]{:S(2)}) async-start(), calls=%async_computation.19 | async-start | bytes 442368
  767.0 282.1 %reduce-scatter.27.cloned.1.call-start = ((), (), s32[]{:S(2)}) async-start(), calls=%async_computation.16 | async-start | bytes 2654208 | tf_op jit(solution)/shard_map/reduce_scatter | solution.py:292
  771.5 349.7 %reduce-scatter.29.cloned.1.call-start = ((), (), s32[]{:S(2)}) async-start(), calls=%async_computation.17 | async-start | bytes 2654208 | tf_op jit(solution)/shard_map/reduce_scatter | solution.py:293
  776.3 417.0 %reduce-scatter.25.cloned.1.call-start = ((), (), s32[]{:S(2)}) async-start(), calls=%async_computation.15 | async-start | bytes 2654208 | tf_op jit(solution)/shard_map/reduce_scatter | solution.py:290
  (145 other events, 1514.7 us)
Sparse Core Ops, SparseCore 0:
  371.3 31.0 all-reduce.11
  470.0 32.2 all-reduce.9
  720.3 37.1 all-reduce.7
Sparse Core Ops, SparseCore 1:
  373.8 38.6 all-gather.8
  414.5 40.0 all-gather.10
  513.7 65.8 reduce-scatter.22
  583.4 64.5 reduce-scatter.20
  651.4 64.4 reduce-scatter.18
  724.6 61.4 reduce-scatter.36
  789.2 60.5 reduce-scatter.30
  852.9 60.4 reduce-scatter.34
  916.5 60.5 reduce-scatter.32
  981.2 67.8 reduce-scatter.26
  1053.0 68.0 reduce-scatter.28
  1125.2 68.0 reduce-scatter.24
where the time goes:
time: 1210 us; the launch traced here: 1200 us
  waiting for transfers between devices  674 us (56%)
  blocking collectives  359 us (30%)
  matrix products  68.5 us (6%)
  other arithmetic  54.7 us (5%)
  local copies, waits for them, and re-layouts  25.1 us (2%)
  between operations  18.4 us (2%)
    reduce_scatter x3, waiting for transfers between devices, per_device(): lax.psum_scatter(terms.reshape(row_len, 2 * local_width), 'seq', scatter_...  175 us
    unnamed x19, waiting for transfers between devices  158 us
    all_gather x3, blocking collectives, per_device(): lax.all_gather(key_rows, 'seq', axis=0, tiled=True)  81 us
    all_gather x3, blocking collectives, per_device(): lax.all_gather(value_rows, 'seq', axis=0, tiled=True)  80.7 us
    psum x3, waiting for transfers between devices, head_total(): lax.psum(partial_sum.astype(jnp.bfloat16), 'head').astype(jnp.float32)  80.1 us
    reduce_scatter x1, waiting for transfers between devices, per_device(): lax.psum_scatter(sum_qkv, 'seq', scatter_dimension=0, tiled=True)  72.2 us
    reduce_scatter x1, waiting for transfers between devices, per_device(): lax.psum_scatter(sum_down, 'seq', scatter_dimension=1, tiled=True)  72 us
    reduce_scatter x1, waiting for transfers between devices, per_device(): lax.psum_scatter(sum_up, 'seq', scatter_dimension=0, tiled=True)  70.6 us
  transfers between devices with their start and end apart: 15, of which 14 were waited for; matrix products, arithmetic and copies ran while one was open for 6% of the time, Pallas kernels for 0%

commit v1 on v0

--- a/solution.py
+++ b/solution.py
@@ -3,7 +3,11 @@
 
 import jax
 import jax.numpy as jnp
+import ml_dtypes
+import numpy as np
 from jax import lax
+from jax.experimental import pallas as pl
+from jax.experimental.pallas import tpu as pltpu
 from jax.sharding import PartitionSpec as P
 
 HDIM = 48
@@ -311,6 +315,727 @@
     )
 
 
+NEG = 1792.0
+ROOT = 1.0 / math.sqrt(HDIM)
+BF = jnp.bfloat16
+F32 = jnp.float32
+MESH = pl.DeviceIdType.MESH
+LEVELS = [math.sqrt(HDIM) * math.log((b + 1) / b) for b in range(1, BRANCHES)]
+LEVEL_HIGH = [float(np.asarray(v, ml_dtypes.bfloat16)) for v in LEVELS]
+LEVEL_LOW = [v - w for v, w in zip(LEVELS, LEVEL_HIGH)]
+
+
+def nn(a, b):
+    return lax.dot_general(a, b, (((1,), (0,)), ((), ())), preferred_element_type=F32)
+
+
+def nt(a, b):
+    return lax.dot_general(a, b, (((1,), (1,)), ((), ())), preferred_element_type=F32)
+
+
+def tn(a, b):
+    return lax.dot_general(a, b, (((0,), (0,)), ((), ())), preferred_element_type=F32)
+
+
+def tt(a, b):
+    return lax.dot_general(a, b, (((0,), (1,)), ((), ())), preferred_element_type=F32)
+
+
+def four(index, values):
+    return jnp.where(
+        index == 0,
+        values[0],
+        jnp.where(index == 1, values[1], jnp.where(index == 2, values[2], values[3])),
+    )
+
+
+def pair_features(pos, slide, keep, head, for_keys):
+    shape = (16, pos.shape[1])
+    row = lax.broadcasted_iota(jnp.int32, shape, 0)
+    pos = jnp.broadcast_to(pos, shape)
+    slide = jnp.broadcast_to(slide, shape)
+    level = jnp.where(row >= 8, row - 8, row - 4)
+    on = jnp.bitwise_and(pos - head, four(level, [1, 3, 7, 15])) == 0
+    on = on & (row < 12)
+    if for_keys:
+        keep = jnp.broadcast_to(keep, shape)
+        size = jnp.where(row < 8, four(level, LEVEL_HIGH), four(level, LEVEL_LOW))
+        other = jnp.where(slide != row, -NEG, 0.0)
+        padding = jnp.where(keep > 0.0, 0.0, -NEG)
+    else:
+        size = jnp.ones(shape, F32)
+        other = jnp.where(slide == row, 1.0, 0.0)
+        padding = jnp.ones(shape, F32)
+    value = jnp.where(row < 3, other, jnp.where(row == 3, padding, jnp.where(on, size, 0.0)))
+    return value.astype(BF)
+
+
+def layer_kernel(*refs, names):
+    r_ = dict(zip(names, refs))
+
+    class N:
+        pass
+
+    g = N()
+    for k, v in r_.items():
+        setattr(g, k, v)
+    s = lax.axis_index("seq")
+    h = lax.axis_index("head")
+    z, y = lax.div(s, 2), lax.rem(s, 2)
+    x, c = lax.div(h, 2), lax.rem(h, 2)
+    a, j = lax.div(s, 4), lax.rem(s, 4)
+    sib = (s, h + 1 - 2 * c)
+    xp = (s, lax.rem(h + 2, 4))
+    yp = (s + 1 - 2 * y, h)
+    zs = [lax.rem(z + d, 4) for d in (1, 2, 3)]
+    zm = [(2 * q + y, h) for q in zs]
+    part = [(4 * c + i, 2 * x + a) for i in range(4)]
+    own = [(a == c) & (j == i) for i in range(4)]
+    is_own = jnp.where(a == c, 1, 0)
+    head = 8 * x + s
+    R = 3
+    T = 128
+
+    def rdma(src, dst, ss, rs, dev):
+        return pltpu.make_async_remote_copy(
+            src_ref=src, dst_ref=dst, send_sem=ss, recv_sem=rs, device_id=dev, device_id_type=MESH
+        )
+
+    def not_own(i):
+        return jnp.logical_not(own[i])
+
+    def lanes(r, n=128):
+        return pl.ds(pl.multiple_of(n * r, n), n)
+
+    def rows(r, n=128):
+        return pl.ds(pl.multiple_of(n * r, n), n)
+
+    def half(r, who):
+        return pl.ds(pl.multiple_of(T * r + 64 * who, 64), 64)
+
+    bar = pltpu.get_barrier_semaphore()
+    for dev in [sib, xp, yp] + zm:
+        pl.semaphore_signal(bar, inc=1, device_id=dev, device_id_type=MESH)
+    for i in range(4):
+
+        @pl.when(not_own(i))
+        def _():
+            pl.semaphore_signal(bar, inc=1, device_id=part[i], device_id_type=MESH)
+
+    pl.semaphore_wait(bar, 10 - is_own)
+
+    W = [g.wq, g.wo, g.wu, g.wd]
+
+    def ag_start(p):
+        w = W[p]
+        for t, dev in enumerate([yp] + zm):
+            rdma(w.at[s], w.at[s], g.ag_s.at[p, t], g.ag_r.at[p, s], dev).start()
+
+    def ag_forward(p):
+        w = W[p]
+        for t in range(3):
+            k = zm[t][0]
+            rdma(w.at[k], w.at[k], g.ag_s.at[p, 4 + t], g.ag_r.at[p, k], zm[t]).wait_recv()
+            rdma(w.at[k], w.at[k], g.ag_s.at[p, 4 + t], g.ag_r.at[p, k], yp).start()
+
+    def ag_wait(p):
+        w = W[p]
+        for q in range(4):
+            k = 2 * q + 1 - y
+            rdma(w.at[k], w.at[k], g.ag_s.at[p, 0], g.ag_r.at[p, k], yp).wait_recv()
+
+    def ag_drain(p):
+        w = W[p]
+        for t in range(7):
+            rdma(w.at[s], w.at[s], g.ag_s.at[p, t], g.ag_r.at[p, s], yp).wait_send()
+
+    g.wq[s] = g.in_wq[...]
+    ag_start(0)
+    g.wu[s] = g.in_wu[...]
+    g.wo[s] = jnp.transpose(g.in_wo[...])
+    g.wd[s] = jnp.transpose(g.in_wd[...])
+
+    lane = lax.broadcasted_iota(jnp.int32, (1, 768), 1)
+    freq = jnp.exp(
+        -math.log(10000.0) * lax.rem(lane, 192).astype(F32) / 192.0
+    )
+    for r in range(R):
+        col = jnp.transpose(g.in_crd[r])
+        pieces = []
+        for t in range(6):
+            f = freq[:, 128 * t : 128 * t + 128]
+            ang = col[:, (0 if t < 3 else 1) : (1 if t < 3 else 2)] * f
+            if t % 3 == 0:
+                pieces.append(jnp.sin(ang))
+            elif t % 3 == 2:
+                pieces.append(jnp.cos(ang))
+            else:
+                low_half = lax.broadcasted_iota(jnp.int32, (T, 128), 1) < 64
+                pieces.append(jnp.where(low_half, jnp.sin(ang), jnp.cos(ang)))
+        v = g.in_tok[rows(r), :].astype(F32) + jnp.concatenate(pieces, axis=1)
+        g.inp[rows(r), :] = v
+        v = v - jnp.mean(v, axis=1, keepdims=True)
+        rstd = lax.rsqrt(jnp.mean(v * v, axis=1, keepdims=True) + EPSILON)
+        g.n1[rows(r), :] = v * rstd
+        g.rstd1[rows(r), :] = rstd
+        g.cotT[:, 128 * r : 128 * r + 128] = jnp.transpose(g.in_cot[rows(r), :])
+    g.sums[...] = jnp.zeros_like(g.sums)
+
+    ag_forward(0)
+    ag_start(1)
+    ag_start(2)
+    ag_wait(0)
+
+    par = jnp.concatenate([g.wq[k, 96:112, 0:96].astype(F32) for k in range(8)], axis=1)
+    g.par[...] = par
+    g1, s1, ob0, ob1 = par[1:2], par[3:4], par[4:5], par[5:6]
+    g0 = par[0:1]
+    qvb = g.in_qvb[...].astype(F32)
+    qkv_bias = jnp.concatenate([qvb[0:1], jnp.zeros((1, 192), F32), qvb[1:2]], axis=1)
+
+    def send_part(i, r, src, dst, ss, rs):
+        @pl.when(not_own(i))
+        def _():
+            rdma(src.at[i, r], dst.at[j, r], ss.at[i, r], rs.at[j, r], part[i]).start()
+
+        @pl.when(own[i])
+        def _():
+            dst[i, r] = src[i, r]
+
+    def wait_part(i, r, dst, ss, rs):
+        @pl.when(not_own(i))
+        def _():
+            rdma(dst.at[i, r], dst.at[i, r], ss.at[i, r], rs.at[i, r], part[i]).wait_recv()
+
+    def drain_part(i, r, src, ss, rs):
+        @pl.when(not_own(i))
+        def _():
+            rdma(src.at[i, r], src.at[i, r], ss.at[i, r], rs.at[i, r], part[i]).wait_send()
+
+    for r in range(R):
+        nr = (g.n1[rows(r), :] * g0 + par[2:3]).astype(BF)
+        g.nrmT[:, 128 * r : 128 * r + 128] = jnp.transpose(nr)
+        proj = nn(nr, g.wq[:, 0:96, :].reshape(768, 576)) + qkv_bias
+        projT = jnp.transpose(proj).astype(BF)
+        for i in range(4):
+            for t in range(3):
+                g.snA[i, r, 48 * t : 48 * t + 48, :] = projT[192 * t + 48 * i : 192 * t + 48 * i + 48]
+            send_part(i, r, g.snA, g.rcA, g.qa_s, g.qa_r)
+
+    ag_forward(1)
+    ag_start(3)
+
+    def slide_of_row(r, pos):
+        b0 = g.in_len[r, 0]
+        b1 = b0 + g.in_len[r, 1]
+        return jnp.where(pos >= b0, 1, 0) + jnp.where(pos >= b1, 1, 0)
+
+    ones_rows = jnp.where(lax.broadcasted_iota(jnp.int32, (16, 1024), 0) == 0, 1.0, 0.0).astype(BF)
+
+    def attn_fwd(r):
+        for i in range(4):
+            wait_part(i, r, g.rcA, g.qa_s, g.qa_r)
+            rdma(
+                g.rcA.at[i, r, pl.ds(48, 96)], g.sbA.at[i, r], g.sa_s.at[i, r], g.sa_r.at[i, r], sib
+            ).start()
+        iota = lax.broadcasted_iota(jnp.int32, (1, 512), 1)
+        pos_own = 512 * c + iota
+        pos_sib = 512 * (1 - c) + iota
+        keep_own = jnp.concatenate(
+            [g.wq[4 * c + i, 96:112, 0:128].astype(F32)[6 + r : 7 + r] for i in range(4)], axis=1
+        )
+        keep_sib = jnp.concatenate(
+            [g.wq[4 * (1 - c) + i, 96:112, 0:128].astype(F32)[6 + r : 7 + r] for i in range(4)], axis=1
+        )
+        pos = jnp.concatenate([pos_own, pos_sib], axis=1)
+        kf = pair_features(
+            pos, slide_of_row(r, pos), jnp.concatenate([keep_own, keep_sib], axis=1), head, True
+        )
+        qf = pair_features(pos_own, slide_of_row(r, pos_own), None, head, False)
+        g.QT[r, 0:48, :] = jnp.concatenate([g.rcA[i, r, 0:48, :] for i in range(4)], axis=1)
+        g.QT[r, 48:64, :] = qf
+        g.KT[r, 48:64, :] = kf
+        g.VT[r, 48:64, :] = ones_rows
+        for i in range(4):
+            g.KT[r, 0:48, 128 * i : 128 * i + 128] = g.rcA[i, r, 48:96, :]
+            g.VT[r, 0:48, 128 * i : 128 * i + 128] = g.rcA[i, r, 96:144, :]
+        for i in range(4):
+            rdma(g.sbA.at[i, r], g.sbA.at[i, r], g.sa_s.at[i, r], g.sa_r.at[i, r], sib).wait_recv()
+            g.KT[r, 0:48, 512 + 128 * i : 640 + 128 * i] = g.sbA[i, r, 0:48, :]
+            g.VT[r, 0:48, 512 + 128 * i : 640 + 128 * i] = g.sbA[i, r, 48:96, :]
+        eye = lax.broadcasted_iota(jnp.int32, (256, 256), 0) == lax.broadcasted_iota(
+            jnp.int32, (256, 256), 1
+        )
+        for qc in range(2):
+            q0 = 256 * qc
+            sc = tn(g.KT[r], g.QT[r, :, q0 : q0 + 256])
+            lift = jnp.where(eye, NEG * (1.0 - keep_own[:, q0 : q0 + 256]), 0.0)
+            blocks = [sc[256 * t : 256 * t + 256] for t in range(4)]
+            blocks[qc] = blocks[qc] + lift
+            sc = jnp.concatenate(blocks, axis=0)
+            peak = jnp.max(sc, axis=0, keepdims=True)
+            pb = jnp.exp((sc - peak) * ROOT).astype(BF)
+            g.P[r, :, q0 : q0 + 256] = pb
+            o = nn(g.VT[r], pb)
+            inv = 1.0 / o[48:49]
+            o = o[0:48] * inv
+            g.O[r, :, q0 : q0 + 256] = o
+            g.inv[r, :, q0 : q0 + 256] = jnp.broadcast_to(inv, (8, 256))
+            for u in range(2):
+                i = 2 * qc + u
+                g.snO[i, r] = o[:, 128 * u : 128 * u + 128].astype(BF)
+                send_part(i, r, g.snO, g.rcO, g.o_s, g.o_r)
+
+    attn_fwd(0)
+    ag_forward(2)
+    attn_fwd(1)
+    attn_fwd(2)
+    ag_forward(3)
+
+    def ps_start(kind, r, part_sum):
+        g.ps[kind, r] = part_sum.astype(BF)
+        rdma(
+            g.ps.at[kind, r, pl.ds(pl.multiple_of(64 * (1 - c), 64), 64)],
+            g.psA.at[kind, r],
+            g.ps_s.at[kind, r, 0],
+            g.ps_r.at[kind, r, 0],
+            sib,
+        ).start()
+
+    def ps_mid(kind, r):
+        dst = g.psA.at[kind, r]
+        rdma(dst, dst, g.ps_s.at[kind, r, 0], g.ps_r.at[kind, r, 0], sib).wait_recv()
+        mine = g.ps[kind, r, pl.ds(pl.multiple_of(64 * c, 64), 64), :].astype(F32)
+        g.psH[kind, r] = (mine + g.psA[kind, r].astype(F32)).astype(BF)
+        rdma(
+            g.psH.at[kind, r], g.psB.at[kind, r], g.ps_s.at[kind, r, 1], g.ps_r.at[kind, r, 1], xp
+        ).start()
+
+    def ps_end(kind, r):
+        dst = g.psB.at[kind, r]
+        rdma(dst, dst, g.ps_s.at[kind, r, 1], g.ps_r.at[kind, r, 1], xp).wait_recv()
+        return g.psH[kind, r].astype(F32) + g.psB[kind, r].astype(F32)
+
+    def share_start(ref, r, ss, rs):
+        rdma(ref.at[half(r, c)], ref.at[half(r, c)], ss.at[r], rs.at[r], sib).start()
+
+    def share_wait(ref, r, ss, rs):
+        dst = ref.at[half(r, 1 - c)]
+        rdma(dst, dst, ss.at[r], rs.at[r], sib).wait_recv()
+
+    ag_wait(1)
+    for r in range(R):
+        for i in range(4):
+            wait_part(i, r, g.rcO, g.o_s, g.o_r)
+            g.attT[48 * i : 48 * i + 48, 128 * r : 128 * r + 128] = g.rcO[i, r]
+        att = jnp.transpose(g.attT[:, 128 * r : 128 * r + 128])
+        ps_start(0, r, nt(att, g.wo[...].reshape(768, 192)))
+        if r > 0:
+            ps_mid(0, r - 1)
+    ps_mid(0, R - 1)
+    ag_wait(2)
+    ag_wait(3)
+
+    def second_norm(r):
+        v = g.inp[half(r, c), :] + ps_end(0, r) + ob0
+        g.mid[r] = v
+        v = v - jnp.mean(v, axis=1, keepdims=True)
+        rstd = lax.rsqrt(jnp.mean(v * v, axis=1, keepdims=True) + EPSILON)
+        v = v * rstd
+        g.n2[r] = v
+        g.rstd2[r] = rstd
+        g.ntk[half(r, c), :] = (v * g1 + s1).astype(BF)
+        share_start(g.ntk, r, g.nt_s, g.nt_r)
+
+    up_bias = g.in_upb[...].astype(F32)
+
+    def feed_forward(r):
+        share_wait(g.ntk, r, g.nt_s, g.nt_r)
+        pre = nn(g.ntk[rows(r), :], g.wu[...].reshape(768, 768)) + up_bias
+        cdf = 0.5 * (1.0 + lax.erf(pre * (1.0 / math.sqrt(2.0))))
+        pdf = jnp.exp(-0.5 * pre * pre) * (1.0 / math.sqrt(2.0 * math.pi))
+        g.act[rows(r), :] = (pre * cdf).astype(BF)
+        gact = nn(g.in_cot[rows(r), :], g.wd[...].reshape(768, 768))
+        g.gp[rows(r), :] = (gact * (cdf + pre * pdf)).astype(BF)
+        ps_start(1, r, nt(g.gp[rows(r), :], g.wu[...].reshape(768, 768)))
+
+    second_norm(0)
+    second_norm(1)
+    feed_forward(0)
+    second_norm(2)
+    feed_forward(1)
+    ps_mid(1, 0)
+    feed_forward(2)
+    ps_mid(1, 1)
+
+    def block(p, k):
+        b = pl.ds(pl.multiple_of(96 * k, 96), 96)
+        if p == 0:
+            return nt(g.nrmT[b, :], g.gpT[...])
+        if p == 1:
+            return nt(g.gbT[b, :], g.attT[...])
+        if p == 2:
+            return nn(g.ntT[b, :], g.gp[...])
+        return nn(g.cotT[b, :], g.act[...])
+
+    L1S = [g.l1s0, g.l1s1, g.l1s2, g.l1s3]
+    L1R = [g.l1r0, g.l1r1, g.l1r2, g.l1r3]
+    L2S = [g.l2s0, g.l2s1, g.l2s2, g.l2s3]
+    L2R = [g.l2r0, g.l2r1, g.l2r2, g.l2r3]
+    ACC = [g.out_gqkv, g.out_gout, g.out_gup, g.out_gdown]
+
+    def rs_first(p):
+        def step(q, _):
+            L1S[p][q] = block(p, 2 * q + 1 - y).astype(BF)
+            rdma(L1S[p].at[q], L1R[p].at[q], g.l1_s.at[p, q], g.l1_r.at[p, q], yp).start()
+            return 0
+
+        lax.fori_loop(0, 4, step, 0)
+
+    def rs_second(p):
+        def step(t, _):
+            q = lax.rem(z + t, 4)
+            dst = L1R[p].at[q]
+            rdma(dst, dst, g.l1_s.at[p, q], g.l1_r.at[p, q], yp).wait_recv()
+            L2S[p][q] = (block(p, 2 * q + y) + L1R[p][q].astype(F32)).astype(BF)
+            rdma(
+                L2S[p].at[q], L2R[p].at[z], g.l2_s.at[p, q], g.l2_r.at[p, z], (2 * q + y, h)
+            ).start()
+            return 0
+
+        lax.fori_loop(1, 4, step, 0)
+        dst = L1R[p].at[z]
+        rdma(dst, dst, g.l1_s.at[p, z], g.l1_r.at[p, z], yp).wait_recv()
+        ACC[p][...] = block(p, s) + L1R[p][z].astype(F32)
+
+    def rs_third(p):
+        for t in (1, 2, 3):
+            q = lax.rem(z + t, 4)
+            dst = L2R[p].at[q]
+            rdma(dst, dst, g.l2_s.at[p, q], g.l2_r.at[p, q], yp).wait_recv()
+            ACC[p][...] += dst[...].astype(F32)
+
+    def rs_drain(p):
+        for q in range(4):
+            rdma(L1S[p].at[q], L1R[p].at[q], g.l1_s.at[p, q], g.l1_r.at[p, q], yp).wait_send()
+        for t in (1, 2, 3):
+            q = lax.rem(z + t, 4)
+            rdma(L2S[p].at[q], L2R[p].at[q], g.l2_s.at[p, q], g.l2_r.at[p, q], yp).wait_send()
+
+    rs_first(3)
+    ps_mid(1, 2)
+    g.ntT[...] = jnp.transpose(g.ntk[...])
+    rs_first(2)
+
+    def add_sum(row, value):
+        g.sums[row : row + 1, :] += jnp.sum(value, axis=0, keepdims=True)
+
+    def norm_back(grad, n, rstd, gain):
+        e = grad * gain
+        return rstd * (
+            e - jnp.mean(e, axis=1, keepdims=True) - n * jnp.mean(e * n, axis=1, keepdims=True)
+        )
+
+    def second_back(r):
+        gn = ps_end(1, r)
+        n = g.n2[r]
+        cot = g.in_cot[half(r, c), :].astype(F32)
+        gm = cot + norm_back(gn, n, g.rstd2[r], g1)
+        g.gm[r] = gm
+        gb = gm.astype(BF)
+        g.gb[half(r, c), :] = gb
+        share_start(g.gb, r, g.gb_s, g.gb_r)
+        add_sum(1, gn * n)
+        add_sum(3, gn)
+        add_sum(4, gb.astype(F32))
+        add_sum(5, cot)
+
+    def grad_attended(r):
+        share_wait(g.gb, r, g.gb_s, g.gb_r)
+        ga = jnp.transpose(nn(g.gb[rows(r), :], g.wo[...].reshape(768, 192))).astype(BF)
+        for i in range(4):
+            g.snD[i, r] = ga[48 * i : 48 * i + 48]
+            send_part(i, r, g.snD, g.rcD, g.d_s, g.d_r)
+
+    second_back(0)
+    second_back(1)
+    grad_attended(0)
+    second_back(2)
+    grad_attended(1)
+    grad_attended(2)
+
+    for r in range(R):
+        ps_start(2, r, nt(g.act[rows(r), :], g.wd[...].reshape(768, 768)))
+    g.gbT[...] = jnp.transpose(g.gb[...])
+    rs_first(1)
+    for r in range(R):
+        ps_mid(2, r)
+
+    def attn_bwd(r):
+        for i in range(4):
+            wait_part(i, r, g.rcD, g.d_s, g.d_r)
+        dk = None
+        dv = None
+        for qc in range(2):
+            q0 = 256 * qc
+            do = jnp.concatenate([g.rcD[2 * qc, r], g.rcD[2 * qc + 1, r]], axis=1)
+            delta = jnp.sum(do.astype(F32) * g.O[r, :, q0 : q0 + 256], axis=0, keepdims=True)
+            dp = tn(g.VT[r, 0:48, :], do)
+            pn = g.P[r, :, q0 : q0 + 256].astype(F32) * g.inv[r, 0:1, q0 : q0 + 256]
+            ds = (pn * (dp - delta)).astype(BF)
+            pn = pn.astype(BF)
+            dq = nn(g.KT[r, 0:48, :], ds) * ROOT
+            for u in range(2):
+                g.snG[2 * qc + u, r, 0:48, :] = dq[:, 128 * u : 128 * u + 128].astype(BF)
+            dk_part = nt(g.QT[r, 0:48, q0 : q0 + 256], ds)
+            dv_part = nt(do, pn)
+            dk = dk_part if dk is None else dk + dk_part
+            dv = dv_part if dv is None else dv + dv_part
+        dk = dk * ROOT
+        g.snX[r, 0:48, :] = dk[:, 512:1024]
+        g.snX[r, 48:96, :] = dv[:, 512:1024]
+        rdma(g.snX.at[r], g.rcX.at[r], g.x_s.at[r], g.x_r.at[r], sib).start()
+        g.kvX[r, 0:48, :] = dk[:, 0:512]
+        g.kvX[r, 48:96, :] = dv[:, 0:512]
+
+    def attn_bwd_end(r):
+        rdma(g.rcX.at[r], g.rcX.at[r], g.x_s.at[r], g.x_r.at[r], sib).wait_recv()
+        kv = (g.kvX[r] + g.rcX[r]).astype(BF)
+        for i in range(4):
+            g.snG[i, r, 48:144, :] = kv[:, 128 * i : 128 * i + 128]
+            send_part(i, r, g.snG, g.rcG, g.g_s, g.g_r)
+
+    attn_bwd(0)
+    rs_second(3)
+    attn_bwd_end(0)
+    attn_bwd(1)
+    rs_second(2)
+    attn_bwd_end(1)
+    attn_bwd(2)
+    rs_second(1)
+    attn_bwd_end(2)
+
+    for r in range(R):
+        g.out_tok[half(r, c), :] = (g.mid[r] + ps_end(2, r) + ob1).astype(BF)
+        share_start(g.out_tok, r, g.ot_s, g.ot_r)
+    ones = jnp.ones((8, 384), BF)
+    g.sums[6:7, :] = nn(ones, g.gp[...])[0:1]
+
+    for r in range(R):
+        for i in range(4):
+            wait_part(i, r, g.rcG, g.g_s, g.g_r)
+            for t in range(3):
+                g.gpT[192 * t + 48 * i : 192 * t + 48 * i + 48, 128 * r : 128 * r + 128] = g.rcG[
+                    i, r, 48 * t : 48 * t + 48, :
+                ]
+        ps_start(3, r, tt(g.gpT[:, 128 * r : 128 * r + 128], g.wq[:, 0:96, :].reshape(768, 576)))
+        if r > 0:
+            ps_mid(3, r - 1)
+    rs_first(0)
+    ps_mid(3, R - 1)
+    g.sums[7:8, 0:576] = nt(ones, g.gpT[...])[0:1]
+
+    rs_third(3)
+    rs_third(2)
+    rs_third(1)
+
+    def first_back(r):
+        gn = ps_end(3, r)
+        n = g.n1[half(r, c), :]
+        gt = g.gm[r] + norm_back(gn, n, g.rstd1[half(r, c), :], g0)
+        g.out_gtok[half(r, c), :] = gt.astype(BF)
+        share_start(g.out_gtok, r, g.gt_s, g.gt_r)
+        add_sum(0, gn * n)
+        add_sum(2, gn)
+
+    for r in range(R):
+        first_back(r)
+    rdma(g.sums, g.sumA, g.sm_s.at[0], g.sm_r.at[0], sib).start()
+    rs_second(0)
+    rdma(g.sumA, g.sumA, g.sm_s.at[0], g.sm_r.at[0], sib).wait_recv()
+    both = lax.broadcasted_iota(jnp.int32, (8, 768), 0) < 6
+    g.sumB[...] = g.sums[...] + jnp.where(both, g.sumA[...], 0.0)
+    rdma(g.sumB, g.sumC, g.sm_s.at[1], g.sm_r.at[1], yp).start()
+    rdma(g.sumC, g.sumC, g.sm_s.at[1], g.sm_r.at[1], yp).wait_recv()
+    g.sumD[z] = g.sumB[...] + g.sumC[...]
+    for t in range(3):
+        rdma(g.sumD.at[z], g.sumD.at[z], g.sm_s.at[2 + t], g.sm_r.at[2 + z], zm[t]).start()
+    rs_third(0)
+    for t in range(3):
+        q = zs[t]
+        rdma(g.sumD.at[q], g.sumD.at[q], g.sm_s.at[2 + t], g.sm_r.at[2 + q], zm[t]).wait_recv()
+    total = g.sumD[0] + g.sumD[1] + g.sumD[2] + g.sumD[3]
+    g.out_sums[...] = total
+    for k in range(8):
+        g.cut[k] = total[:, 96 * k : 96 * k + 96]
+    g.out_cut[...] = g.cut[s]
+
+    for r in range(R):
+        share_wait(g.out_tok, r, g.ot_s, g.ot_r)
+        share_wait(g.out_gtok, r, g.gt_s, g.gt_r)
+    for p in range(4):
+        ag_drain(p)
+        rs_drain(p)
+    for r in range(R):
+        for i in range(4):
+            drain_part(i, r, g.snA, g.qa_s, g.qa_r)
+            drain_part(i, r, g.snO, g.o_s, g.o_r)
+            drain_part(i, r, g.snD, g.d_s, g.d_r)
+            drain_part(i, r, g.snG, g.g_s, g.g_r)
+            rdma(g.sbA.at[i, r], g.sbA.at[i, r], g.sa_s.at[i, r], g.sa_r.at[i, r], sib).wait_send()
+        rdma(g.snX.at[r], g.rcX.at[r], g.x_s.at[r], g.x_r.at[r], sib).wait_send()
+        for kind in range(4):
+            for t in range(2):
+                rdma(
+                    g.psH.at[kind, r], g.psB.at[kind, r], g.ps_s.at[kind, r, t], g.ps_r.at[kind, r, t], xp
+                ).wait_send()
+        for ref, ss, rs in (
+            (g.ntk, g.nt_s, g.nt_r),
+            (g.gb, g.gb_s, g.gb_r),
+            (g.out_tok, g.ot_s, g.ot_r),
+            (g.out_gtok, g.gt_s, g.gt_r),
+        ):
+            rdma(ref.at[half(r, c)], ref.at[half(r, c)], ss.at[r], rs.at[r], sib).wait_send()
+    rdma(g.sums, g.sumA, g.sm_s.at[0], g.sm_r.at[0], sib).wait_send()
+    rdma(g.sumB, g.sumC, g.sm_s.at[1], g.sm_r.at[1], yp).wait_send()
+    for t in range(3):
+        rdma(g.sumD.at[z], g.sumD.at[z], g.sm_s.at[2 + t], g.sm_r.at[2 + z], zm[t]).wait_send()
+
+
+def fast_device(
+    tokens, cotangent, lengths, coords, keep_mask, ln_gains, ln_shifts, out_bias,
+    w_qkv, qv_bias, w_out, w_up, up_bias, w_down,
+):
+    small = jnp.concatenate([ln_gains, ln_shifts, out_bias], axis=0)
+    small = jnp.pad(small, ((0, 0), (0, 480)))
+    keep = jnp.pad(keep_mask.astype(BF), ((0, 7), (0, 448)))
+    shard = jnp.concatenate([w_qkv.reshape(96, 576), small, keep], axis=0)
+    crd = jnp.pad(jnp.transpose(coords, (1, 0, 2)).astype(F32), ((0, 0), (0, 6), (0, 0)))
+    inputs = [
+        ("in_tok", tokens.reshape(384, 768)),
+        ("in_cot", cotangent.reshape(384, 768)),
+        ("in_len", lengths),
+        ("in_crd", crd),
+        ("in_wq", shard),
+        ("in_qvb", qv_bias),
+        ("in_wo", w_out),
+        ("in_wu", w_up),
+        ("in_upb", up_bias.reshape(1, 768)),
+        ("in_wd", w_down),
+    ]
+    outputs = [
+        ("out_tok", (384, 768), BF),
+        ("out_gtok", (384, 768), BF),
+        ("out_gqkv", (96, 576), F32),
+        ("out_gout", (96, 192), F32),
+        ("out_gup", (96, 768), F32),
+        ("out_gdown", (96, 768), F32),
+        ("out_sums", (8, 768), F32),
+        ("out_cut", (8, 96), F32),
+    ]
+    vm = [
+        ("wq", (8, 112, 576), BF),
+        ("wo", (8, 96, 192), BF),
+        ("wu", (8, 96, 768), BF),
+        ("wd", (8, 96, 768), BF),
+        ("inp", (384, 768), F32),
+        ("n1", (384, 768), F32),
+        ("rstd1", (384, 1), F32),
+        ("cotT", (768, 384), BF),
+        ("nrmT", (768, 384), BF),
+        ("par", (16, 768), F32),
+        ("sums", (8, 768), F32),
+        ("sumA", (8, 768), F32),
+        ("sumB", (8, 768), F32),
+        ("sumC", (8, 768), F32),
+        ("sumD", (4, 8, 768), F32),
+        ("cut", (8, 8, 96), F32),
+        ("snA", (4, 3, 144, 128), BF),
+        ("rcA", (4, 3, 144, 128), BF),
+        ("sbA", (4, 3, 96, 128), BF),
+        ("QT", (3, 64, 512), BF),
+        ("KT", (3, 64, 1024), BF),
+        ("VT", (3, 64, 1024), BF),
+        ("P", (3, 1024, 512), BF),
+        ("O", (3, 48, 512), F32),
+        ("inv", (3, 8, 512), F32),
+        ("snO", (4, 3, 48, 128), BF),
+        ("rcO", (4, 3, 48, 128), BF),
+        ("snD", (4, 3, 48, 128), BF),
+        ("rcD", (4, 3, 48, 128), BF),
+        ("snG", (4, 3, 144, 128), BF),
+        ("rcG", (4, 3, 144, 128), BF),
+        ("snX", (3, 96, 512), F32),
+        ("rcX", (3, 96, 512), F32),
+        ("kvX", (3, 96, 512), F32),
+        ("attT", (192, 384), BF),
+        ("gpT", (576, 384), BF),
+        ("ps", (4, 3, 128, 768), BF),
+        ("psA", (4, 3, 64, 768), BF),
+        ("psH", (4, 3, 64, 768), BF),
+        ("psB", (4, 3, 64, 768), BF),
+        ("mid", (3, 64, 768), F32),
+        ("n2", (3, 64, 768), F32),
+        ("rstd2", (3, 64, 1), F32),
+        ("gm", (3, 64, 768), F32),
+        ("ntk", (384, 768), BF),
+        ("ntT", (768, 384), BF),
+        ("act", (384, 768), BF),
+        ("gp", (384, 768), BF),
+        ("gb", (384, 768), BF),
+        ("gbT", (768, 384), BF),
+    ]
+    for p, width in enumerate((576, 192, 768, 768)):
+        for kind in ("l1s", "l1r", "l2s", "l2r"):
+            vm.append((f"{kind}{p}", (4, 96, width), BF))
+    sems = [
+        ("ag_s", (4, 7)), ("ag_r", (4, 8)),
+        ("qa_s", (4, 3)), ("qa_r", (4, 3)),
+        ("sa_s", (4, 3)), ("sa_r", (4, 3)),
+        ("o_s", (4, 3)), ("o_r", (4, 3)),
+        ("d_s", (4, 3)), ("d_r", (4, 3)),
+        ("g_s", (4, 3)), ("g_r", (4, 3)),
+        ("x_s", (3,)), ("x_r", (3,)),
+        ("ps_s", (4, 3, 2)), ("ps_r", (4, 3, 2)),
+        ("nt_s", (3,)), ("nt_r", (3,)),
+        ("gb_s", (3,)), ("gb_r", (3,)),
+        ("ot_s", (3,)), ("ot_r", (3,)),
+        ("gt_s", (3,)), ("gt_r", (3,)),
+        ("l1_s", (4, 4)), ("l1_r", (4, 4)),
+        ("l2_s", (4, 4)), ("l2_r", (4, 4)),
+        ("sm_s", (8,)), ("sm_r", (8,)),
+    ]
+    names = [n for n, _ in inputs] + [o[0] for o in outputs] + [v[0] for v in vm] + [n for n, _ in sems]
+    vmem = pl.BlockSpec(memory_space=pltpu.VMEM)
+    out = pl.pallas_call(
+        partial(layer_kernel, names=names),
+        out_shape=[jax.ShapeDtypeStruct(shape, dtype) for _, shape, dtype in outputs],
+        in_specs=[
+            pl.BlockSpec(memory_space=pltpu.SMEM) if n == "in_len" else vmem for n, _ in inputs
+        ],
+        out_specs=[vmem] * len(outputs),
+        scratch_shapes=[pltpu.VMEM(shape, dtype) for _, shape, dtype in vm]
+        + [pltpu.SemaphoreType.DMA(shape) for _, shape in sems],
+        compiler_params=pltpu.CompilerParams(
+            collective_id=0, has_side_effects=True, vmem_limit_bytes=60 * 1024 * 1024
+        ),
+    )(*[v for _, v in inputs])
+    out_tok, out_gtok, gqkv, gout, gup, gdown, sums, cut = out
+    return (
+        out_tok.reshape(3, 128, 768),
+        out_gtok.reshape(3, 128, 768),
+        cut[0:2],
+        cut[2:4],
+        cut[4:6],
+        gqkv.reshape(96, 3, 192),
+        jnp.stack([sums[7, 0:192], sums[7, 384:576]]),
+        jnp.transpose(gout),
+        gup,
+        sums[6],
+        jnp.transpose(gdown),
+    )
+
+
 def solution(mesh):
     placed = (
         P(None, "seq", None),
@@ -328,8 +1053,15 @@
         P("head"),
         P("head", "seq"),
     )
-    return jax.shard_map(
-        per_device,
+    layout = (mesh.shape["seq"], mesh.shape["head"])
+
+    def step(tokens, *others):
+        one_kernel = layout == (8, 4) and tokens.shape == (3, 1024, 768)
+        return over(fast_device if one_kernel else per_device)(tokens, *others)
+
+    def over(device):
+        return jax.shard_map(
+        device,
         mesh=mesh,
         in_specs=placed,
         out_specs=(
@@ -347,3 +1079,5 @@
         ),
         check_vma=False,
     )
+
+    return step

time: 1210 us -> 189 us (0.16)
  waiting for transfers between devices: 674 us -> 0 us
  blocking collectives: 359 us -> 0 us
  Pallas kernels: 0 us -> 171 us
  matrix products: 68.5 us -> 0 us
  other arithmetic: 54.7 us -> 1.28 us
  between operations: 18.4 us -> 0.71 us
    reduce_scatter x6 -> x0, waiting for transfers between devices: 390 us -> none  [the longest x3 175 us: per_device(): lax.psum_scatter(terms.reshape(row_len, 2 * local_width), 'seq', scatter_...]
    all_gather x14 -> x0, blocking collectives: 337 us -> none  [the longest x3 81 us: per_device(): lax.all_gather(key_rows, 'seq', axis=0, tiled=True)]
    pallas_call x0 -> x1, Pallas kernels: none -> 171 us  [fast_device(): pl.pallas_call(partial(layer_kernel, names=names), out_shape=[jax.ShapeDt...]
    unnamed x19 -> x0, waiting for transfers between devices: 158 us -> none
    psum x3 -> x0, waiting for transfers between devices: 80.1 us -> none  [head_total(): lax.psum(partial_sum.astype(jnp.bfloat16), 'head').astype(jnp.float32)]
    dot_general x51 -> x0, matrix products: 67 us -> none  [the longest x3 8.34 us: per_device(): jnp.einsum('td,tf->df', normed_two, grad_pre_low, preferred_element_type=...]
    all_gather x2 -> x0, waiting for transfers between devices: 46.6 us -> none  [the longest x1 39.6 us: per_device(): lax.all_gather(w_down, 'seq', axis=1, tiled=True)]
    psum x1 -> x0, blocking collectives: 22.4 us -> none  [per_device(): grad_qvb, grad_upb = lax.psum((sum_qvb, sum_upb), 'seq')]
  transfers between devices with their start and end apart: 15 -> 0, of which waited for: 14 -> 0; matrix products, arithmetic and copies ran while one was open for 6% -> 0% of each run, Pallas kernels for 0% -> 0%
where the time goes in v1:
time: 189 us; the launch traced here: 188 us
  Pallas kernels  171 us (90%)
  local copies, waits for them, and re-layouts  15.3 us (8%)
    pallas_call x1, Pallas kernels, fast_device(): pl.pallas_call(partial(layer_kernel, names=names), out_shape=[jax.ShapeDt...  171 us
    unnamed x32, local copies, waits for them, and re-layouts  10.3 us

profile of v1, /device:TPU:0, one launch (start us, length us, event | category | flops | bytes accessed | tf_op | source)
XLA Modules:
  0.0 188.2 jit_solution(16692167188692593223)
XLA Ops:
  0.6 0.0 copy-start.7
  0.7 0.0 copy-start.6
  0.7 0.7 copy-done.7
  1.3 0.0 copy-done.6
  1.3 0.0 copy-start.8
  1.4 0.7 copy-done.8
  2.0 0.6 reshape.46.refs_8_
  2.6 0.0 copy-start.9
  2.6 0.0 copy-start.10
  2.6 0.0 copy-start.11
  2.6 0.6 pad.12.refs_3_
  3.2 0.1 copy-done.9
  3.3 0.0 copy-done.10
  3.3 0.0 copy-done.11
  3.3 1.1 copy.29
  4.4 0.2 copy.30
  4.5 0.0 copy-start.5
  4.6 0.7 fusion.1.refs_4_
  5.2 0.3 copy-done.5
  5.5 0.8 copy.31.refs_9_
  6.3 170.9 %shard_map.221 = (bf16[384,768]{1,0:T(8,128)(2,1)}, bf16[384,768]{1,0:T(8,128)(2,1)}, f32[96,576]{1,0:T(8,128)}, f32[96,192]{1,0:T(8,128)}, f32[96,768]{1,0:T(8,...) custom-call(bf16[384,768]{1,0:T(8,128)(2,1)} %bitcast.14, bf16[384,768]{1,0:T(8,128)(2,1)} %bitcast.15, ...), custom_call_target="tpu_custom_call" | custom-call | tf_op jit(solution)/shard_map/pallas_call | solution.py:1010
  177.3 0.0 copy-start.4
  177.3 0.8 fusion.7
  178.0 1.3 slice_reduce_fusion
  179.4 0.6 pad_maximum_fusion
  180.0 1.4 fusion.8
  181.3 1.6 copy.34
  182.9 0.0 copy-done.4
  183.0 0.0 copy-start.1
  183.0 0.1 copy.32
  183.1 0.9 copy.33
  184.0 0.0 copy-done.1
  184.0 0.0 copy-start
  184.0 0.8 copy.39
  184.8 0.5 copy-done
  185.3 0.0 copy-start.3
  185.3 0.8 copy.40
  186.1 0.3 copy-done.3
  186.4 0.0 copy-start.2
  186.4 0.7 copy.41
  187.1 0.4 copy-done.2
  187.5 0.7 copy.42
  (3 shorter events, 0.0 us)
Async XLA Ops:
  0.6 0.7 copy-start.7
  0.7 0.7 copy-start.6
  1.3 0.7 copy-start.8
  2.6 0.7 copy-start.9
  2.6 0.7 copy-start.10
  2.6 0.7 copy-start.11
  4.5 1.0 copy-start.5
  177.3 5.7 %copy-start.4 = (f32[96,576]{1,0:T(8,128)S(1)}, f32[96,576]{1,0:T(8,128)}, u32[]{:S(2)}) copy-start(f32[96,576]{1,0:T(8,128)} %get-tuple-element.22) | copy-start | bytes 663556
  183.0 1.1 copy-start.1
  184.0 1.3 copy-start
  185.3 1.1 copy-start.3
  186.4 1.1 copy-start.2

commit v2 on v1

--- a/solution.py
+++ b/solution.py
@@ -387,8 +387,13 @@
     sib = (s, h + 1 - 2 * c)
     xp = (s, lax.rem(h + 2, 4))
     yp = (s + 1 - 2 * y, h)
-    zs = [lax.rem(z + d, 4) for d in (1, 2, 3)]
+    top = lax.div(z, 2)
+    zs = [z + 1 - 2 * lax.rem(z, 2), 2 - top, 3 - 3 * top]
     zm = [(2 * q + y, h) for q in zs]
+    zy = [(2 * q + 1 - y, h) for q in zs]
+    qs = zs + [z]
+    inner = (z == 1) | (z == 2)
+    outer = jnp.logical_not(inner)
     part = [(4 * c + i, 2 * x + a) for i in range(4)]
     own = [(a == c) & (j == i) for i in range(4)]
     is_own = jnp.where(a == c, 1, 0)
@@ -414,7 +419,7 @@
         return pl.ds(pl.multiple_of(T * r + 64 * who, 64), 64)
 
     bar = pltpu.get_barrier_semaphore()
-    for dev in [sib, xp, yp] + zm:
+    for dev in [sib, xp, yp] + zm + zy:
         pl.semaphore_signal(bar, inc=1, device_id=dev, device_id_type=MESH)
     for i in range(4):
 
@@ -422,45 +427,83 @@
         def _():
             pl.semaphore_signal(bar, inc=1, device_id=part[i], device_id_type=MESH)
 
-    pl.semaphore_wait(bar, 10 - is_own)
-
-    W = [g.wq, g.wo, g.wu, g.wd]
-
-    def ag_start(p):
+    W = [g.wq, None, g.wu, g.wd]
+
+    def four_of(name):
+        return [r_[f"{name}{q}"] for q in range(4)]
+
+    AGS, AGR, PSS, PSR = four_of("ag_s"), four_of("ag_r"), four_of("ps_s"), four_of("ps_r")
+    L1SS, L1RS, L2SS, L2RS = four_of("l1_s"), four_of("l1_r"), four_of("l2_s"), four_of("l2_r")
+
+    def ag_y(p):
         w = W[p]
-        for t, dev in enumerate([yp] + zm):
-            rdma(w.at[s], w.at[s], g.ag_s.at[p, t], g.ag_r.at[p, s], dev).start()
-
-    def ag_forward(p):
+        rdma(w.at[s], w.at[s], AGS[p].at[0], AGR[p].at[s], yp).start()
+
+    def ag_z(p):
         w = W[p]
-        for t in range(3):
-            k = zm[t][0]
-            rdma(w.at[k], w.at[k], g.ag_s.at[p, 4 + t], g.ag_r.at[p, k], zm[t]).wait_recv()
-            rdma(w.at[k], w.at[k], g.ag_s.at[p, 4 + t], g.ag_r.at[p, k], yp).start()
+        for t in range(2):
+            rdma(w.at[s], w.at[s], AGS[p].at[1 + t], AGR[p].at[s], zm[t]).start()
+
+        @pl.when(inner)
+        def _():
+            rdma(w.at[s], w.at[s], AGS[p].at[3], AGR[p].at[s], zm[2]).start()
+
+    def ag_forward(p, t):
+        w = W[p]
+        k = zm[t][0]
+        rdma(w.at[k], w.at[k], AGS[p].at[4 + t], AGR[p].at[k], zm[t]).wait_recv()
+        if t == 2:
+
+            @pl.when(inner)
+            def _():
+                rdma(w.at[k], w.at[k], AGS[p].at[7], AGR[p].at[k], zm[0]).start()
+
+        rdma(w.at[k], w.at[k], AGS[p].at[4 + t], AGR[p].at[k], yp).start()
 
     def ag_wait(p):
         w = W[p]
-        for q in range(4):
+        for q in qs:
             k = 2 * q + 1 - y
-            rdma(w.at[k], w.at[k], g.ag_s.at[p, 0], g.ag_r.at[p, k], yp).wait_recv()
+            rdma(w.at[k], w.at[k], AGS[p].at[0], AGR[p].at[k], yp).wait_recv()
 
     def ag_drain(p):
         w = W[p]
-        for t in range(7):
-            rdma(w.at[s], w.at[s], g.ag_s.at[p, t], g.ag_r.at[p, s], yp).wait_send()
-
-    g.wq[s] = g.in_wq[...]
-    ag_start(0)
+        for t in (0, 1, 2, 4, 5, 6):
+            rdma(w.at[s], w.at[s], AGS[p].at[t], AGR[p].at[s], yp).wait_send()
+
+        @pl.when(inner)
+        def _():
+            for t in (3, 7):
+                rdma(w.at[s], w.at[s], AGS[p].at[t], AGR[p].at[s], yp).wait_send()
+
+    g.wq[s] = jnp.concatenate(
+        [g.in_w3[0], g.in_w3[1], g.in_w3[2], jnp.transpose(g.in_wo[...])], axis=1
+    )
+    g.tmp[...] = jnp.zeros_like(g.tmp)
+    g.tmp[0:2, 0:96] = g.in_lng[...].astype(F32)
+    g.tmp[2:4, 0:96] = g.in_lns[...].astype(F32)
+    g.tmp[4:6, 0:96] = g.in_ob[...].astype(F32)
+    g.tmp[6:9, :] = g.in_keep[...].astype(F32)
+    g.sml[s] = g.tmp[...].astype(BF)
     g.wu[s] = g.in_wu[...]
-    g.wo[s] = jnp.transpose(g.in_wo[...])
-    g.wd[s] = jnp.transpose(g.in_wd[...])
+    g.wd[s] = g.in_wd[...]
+    pl.semaphore_wait(bar, 13 - is_own)
+    others = [yp] + zm + zy
+    for t, dev in enumerate(others):
+        rdma(g.sml.at[s], g.sml.at[s], g.sml_s.at[t], g.sml_r.at[s], dev).start()
+    ag_y(0)
+    ag_z(0)
+    ag_y(2)
+    ag_z(2)
 
     lane = lax.broadcasted_iota(jnp.int32, (1, 768), 1)
     freq = jnp.exp(
         -math.log(10000.0) * lax.rem(lane, 192).astype(F32) / 192.0
     )
     for r in range(R):
-        col = jnp.transpose(g.in_crd[r])
+        col = jnp.transpose(
+            jnp.concatenate([g.in_crd[r].astype(F32), jnp.zeros((6, 128), F32)], axis=0)
+        )
         pieces = []
         for t in range(6):
             f = freq[:, 128 * t : 128 * t + 128]
@@ -481,17 +524,22 @@
         g.cotT[:, 128 * r : 128 * r + 128] = jnp.transpose(g.in_cot[rows(r), :])
     g.sums[...] = jnp.zeros_like(g.sums)
 
-    ag_forward(0)
-    ag_start(1)
-    ag_start(2)
-    ag_wait(0)
-
-    par = jnp.concatenate([g.wq[k, 96:112, 0:96].astype(F32) for k in range(8)], axis=1)
+    for t, dev in enumerate(others):
+        k = dev[0]
+        rdma(g.sml.at[k], g.sml.at[k], g.sml_s.at[t], g.sml_r.at[k], dev).wait_recv()
+    par = jnp.concatenate([g.sml[k].astype(F32)[:, 0:96] for k in range(8)], axis=1)
     g.par[...] = par
     g1, s1, ob0, ob1 = par[1:2], par[3:4], par[4:5], par[5:6]
     g0 = par[0:1]
     qvb = g.in_qvb[...].astype(F32)
     qkv_bias = jnp.concatenate([qvb[0:1], jnp.zeros((1, 192), F32), qvb[1:2]], axis=1)
+    for r in range(R):
+        nr = (g.n1[rows(r), :] * g0 + par[2:3]).astype(BF)
+        g.nrm[rows(r), :] = nr
+        g.nrmT[:, 128 * r : 128 * r + 128] = jnp.transpose(nr)
+    for t in range(3):
+        ag_forward(0, t)
+    ag_wait(0)
 
     def send_part(i, r, src, dst, ss, rs):
         @pl.when(not_own(i))
@@ -513,17 +561,18 @@
             rdma(src.at[i, r], src.at[i, r], ss.at[i, r], rs.at[i, r], part[i]).wait_send()
 
     for r in range(R):
-        nr = (g.n1[rows(r), :] * g0 + par[2:3]).astype(BF)
-        g.nrmT[:, 128 * r : 128 * r + 128] = jnp.transpose(nr)
-        proj = nn(nr, g.wq[:, 0:96, :].reshape(768, 576)) + qkv_bias
+        proj = nn(g.nrm[rows(r), :], g.wq[:, :, 0:576].reshape(768, 576)) + qkv_bias
         projT = jnp.transpose(proj).astype(BF)
         for i in range(4):
             for t in range(3):
                 g.snA[i, r, 48 * t : 48 * t + 48, :] = projT[192 * t + 48 * i : 192 * t + 48 * i + 48]
             send_part(i, r, g.snA, g.rcA, g.qa_s, g.qa_r)
 
-    ag_forward(1)
-    ag_start(3)
+    ag_y(3)
+    for t in range(3):
+        ag_forward(2, t)
+    ag_z(3)
+    g.wo[...] = g.wq[:, :, 576:768].reshape(768, 192)
 
     def slide_of_row(r, pos):
         b0 = g.in_len[r, 0]
@@ -542,10 +591,10 @@
         pos_own = 512 * c + iota
         pos_sib = 512 * (1 - c) + iota
         keep_own = jnp.concatenate(
-            [g.wq[4 * c + i, 96:112, 0:128].astype(F32)[6 + r : 7 + r] for i in range(4)], axis=1
+            [g.sml[4 * c + i].astype(F32)[6 + r : 7 + r] for i in range(4)], axis=1
         )
         keep_sib = jnp.concatenate(
-            [g.wq[4 * (1 - c) + i, 96:112, 0:128].astype(F32)[6 + r : 7 + r] for i in range(4)], axis=1
+            [g.sml[4 * (1 - c) + i].astype(F32)[6 + r : 7 + r] for i in range(4)], axis=1
         )
         pos = jnp.concatenate([pos_own, pos_sib], axis=1)
         kf = pair_features(
@@ -587,33 +636,32 @@
                 send_part(i, r, g.snO, g.rcO, g.o_s, g.o_r)
 
     attn_fwd(0)
-    ag_forward(2)
     attn_fwd(1)
     attn_fwd(2)
-    ag_forward(3)
+    ag_forward(3, 0)
 
     def ps_start(kind, r, part_sum):
         g.ps[kind, r] = part_sum.astype(BF)
         rdma(
             g.ps.at[kind, r, pl.ds(pl.multiple_of(64 * (1 - c), 64), 64)],
             g.psA.at[kind, r],
-            g.ps_s.at[kind, r, 0],
-            g.ps_r.at[kind, r, 0],
+            PSS[kind].at[r, 0],
+            PSR[kind].at[r, 0],
             sib,
         ).start()
 
     def ps_mid(kind, r):
         dst = g.psA.at[kind, r]
-        rdma(dst, dst, g.ps_s.at[kind, r, 0], g.ps_r.at[kind, r, 0], sib).wait_recv()
+        rdma(dst, dst, PSS[kind].at[r, 0], PSR[kind].at[r, 0], sib).wait_recv()
         mine = g.ps[kind, r, pl.ds(pl.multiple_of(64 * c, 64), 64), :].astype(F32)
         g.psH[kind, r] = (mine + g.psA[kind, r].astype(F32)).astype(BF)
         rdma(
-            g.psH.at[kind, r], g.psB.at[kind, r], g.ps_s.at[kind, r, 1], g.ps_r.at[kind, r, 1], xp
+            g.psH.at[kind, r], g.psB.at[kind, r], PSS[kind].at[r, 1], PSR[kind].at[r, 1], xp
         ).start()
 
     def ps_end(kind, r):
         dst = g.psB.at[kind, r]
-        rdma(dst, dst, g.ps_s.at[kind, r, 1], g.ps_r.at[kind, r, 1], xp).wait_recv()
+        rdma(dst, dst, PSS[kind].at[r, 1], PSR[kind].at[r, 1], xp).wait_recv()
         return g.psH[kind, r].astype(F32) + g.psB[kind, r].astype(F32)
 
     def share_start(ref, r, ss, rs):
@@ -623,18 +671,18 @@
         dst = ref.at[half(r, 1 - c)]
         rdma(dst, dst, ss.at[r], rs.at[r], sib).wait_recv()
 
-    ag_wait(1)
     for r in range(R):
         for i in range(4):
             wait_part(i, r, g.rcO, g.o_s, g.o_r)
             g.attT[48 * i : 48 * i + 48, 128 * r : 128 * r + 128] = g.rcO[i, r]
         att = jnp.transpose(g.attT[:, 128 * r : 128 * r + 128])
-        ps_start(0, r, nt(att, g.wo[...].reshape(768, 192)))
+        ps_start(0, r, nt(att, g.wo[...]))
         if r > 0:
             ps_mid(0, r - 1)
+    ag_forward(3, 1)
     ps_mid(0, R - 1)
+    ag_forward(3, 2)
     ag_wait(2)
-    ag_wait(3)
 
     def second_norm(r):
         v = g.inp[half(r, c), :] + ps_end(0, r) + ob0
@@ -649,24 +697,18 @@
 
     up_bias = g.in_upb[...].astype(F32)
 
-    def feed_forward(r):
+    def feed_up(r):
         share_wait(g.ntk, r, g.nt_s, g.nt_r)
         pre = nn(g.ntk[rows(r), :], g.wu[...].reshape(768, 768)) + up_bias
         cdf = 0.5 * (1.0 + lax.erf(pre * (1.0 / math.sqrt(2.0))))
         pdf = jnp.exp(-0.5 * pre * pre) * (1.0 / math.sqrt(2.0 * math.pi))
         g.act[rows(r), :] = (pre * cdf).astype(BF)
+        g.gd[rows(r), :] = cdf + pre * pdf
+
+    def feed_back(r):
         gact = nn(g.in_cot[rows(r), :], g.wd[...].reshape(768, 768))
-        g.gp[rows(r), :] = (gact * (cdf + pre * pdf)).astype(BF)
+        g.gp[rows(r), :] = (gact * g.gd[rows(r), :]).astype(BF)
         ps_start(1, r, nt(g.gp[rows(r), :], g.wu[...].reshape(768, 768)))
-
-    second_norm(0)
-    second_norm(1)
-    feed_forward(0)
-    second_norm(2)
-    feed_forward(1)
-    ps_mid(1, 0)
-    feed_forward(2)
-    ps_mid(1, 1)
 
     def block(p, k):
         b = pl.ds(pl.multiple_of(96 * k, 96), 96)
@@ -682,50 +724,84 @@
     L1R = [g.l1r0, g.l1r1, g.l1r2, g.l1r3]
     L2S = [g.l2s0, g.l2s1, g.l2s2, g.l2s3]
     L2R = [g.l2r0, g.l2r1, g.l2r2, g.l2r3]
-    ACC = [g.out_gqkv, g.out_gout, g.out_gup, g.out_gdown]
-
-    def rs_first(p):
-        def step(q, _):
+    g.acc = [g.acc0, g.acc1, g.out_gup, g.out_gdown]
+
+    def rs_first(p, start=0, stop=4):
+        def step(t, _):
+            q = four(t, qs)
             L1S[p][q] = block(p, 2 * q + 1 - y).astype(BF)
-            rdma(L1S[p].at[q], L1R[p].at[q], g.l1_s.at[p, q], g.l1_r.at[p, q], yp).start()
+            rdma(L1S[p].at[q], L1R[p].at[q], L1SS[p].at[q], L1RS[p].at[q], yp).start()
             return 0
 
-        lax.fori_loop(0, 4, step, 0)
-
-    def rs_second(p):
-        def step(t, _):
-            q = lax.rem(z + t, 4)
-            dst = L1R[p].at[q]
-            rdma(dst, dst, g.l1_s.at[p, q], g.l1_r.at[p, q], yp).wait_recv()
-            L2S[p][q] = (block(p, 2 * q + y) + L1R[p][q].astype(F32)).astype(BF)
-            rdma(
-                L2S[p].at[q], L2R[p].at[z], g.l2_s.at[p, q], g.l2_r.at[p, z], (2 * q + y, h)
-            ).start()
-            return 0
-
-        lax.fori_loop(1, 4, step, 0)
+        lax.fori_loop(start, stop, step, 0)
+
+    def rs_second(p, t):
+        q = zs[t]
+        dst = L1R[p].at[q]
+        rdma(dst, dst, L1SS[p].at[q], L1RS[p].at[q], yp).wait_recv()
+        mine = block(p, 2 * q + y) + L1R[p][q].astype(F32)
+
+        def send():
+            rdma(L2S[p].at[q], L2R[p].at[z], L2SS[p].at[q], L2RS[p].at[z], zm[t]).start()
+
+        if t < 2:
+            L2S[p][q] = mine.astype(BF)
+            send()
+        else:
+            via = L2R[p].at[z]
+
+            @pl.when(outer)
+            def _():
+                L2S[p][q] = mine.astype(BF)
+                rdma(L2S[p].at[q], L2R[p].at[zs[0]], L2SS[p].at[q], L2RS[p].at[zs[0]], zm[0]).start()
+
+            @pl.when(inner)
+            def _():
+                rdma(via, via, L2SS[p].at[q], L2RS[p].at[z], zm[0]).wait_recv()
+                L2S[p][q] = (mine + via[...].astype(F32)).astype(BF)
+                send()
+
+    def rs_own(p):
         dst = L1R[p].at[z]
-        rdma(dst, dst, g.l1_s.at[p, z], g.l1_r.at[p, z], yp).wait_recv()
-        ACC[p][...] = block(p, s) + L1R[p][z].astype(F32)
+        rdma(dst, dst, L1SS[p].at[z], L1RS[p].at[z], yp).wait_recv()
+        g.acc[p][...] = block(p, s) + L1R[p][z].astype(F32)
 
     def rs_third(p):
-        for t in (1, 2, 3):
-            q = lax.rem(z + t, 4)
+        acc = g.acc[p]
+        for t, q in enumerate(zs):
             dst = L2R[p].at[q]
-            rdma(dst, dst, g.l2_s.at[p, q], g.l2_r.at[p, q], yp).wait_recv()
-            ACC[p][...] += dst[...].astype(F32)
+
+            def add(dst=dst, q=q):
+                rdma(dst, dst, L2SS[p].at[q], L2RS[p].at[q], yp).wait_recv()
+                acc[...] += dst[...].astype(F32)
+
+            if t < 2:
+                add()
+            else:
+                pl.when(inner)(add)
+        return acc[...]
 
     def rs_drain(p):
-        for q in range(4):
-            rdma(L1S[p].at[q], L1R[p].at[q], g.l1_s.at[p, q], g.l1_r.at[p, q], yp).wait_send()
-        for t in (1, 2, 3):
-            q = lax.rem(z + t, 4)
-            rdma(L2S[p].at[q], L2R[p].at[q], g.l2_s.at[p, q], g.l2_r.at[p, q], yp).wait_send()
-
+        for q in qs:
+            rdma(L1S[p].at[q], L1R[p].at[q], L1SS[p].at[q], L1RS[p].at[q], yp).wait_send()
+        for q in zs:
+            rdma(L2S[p].at[q], L2R[p].at[q], L2SS[p].at[q], L2RS[p].at[q], yp).wait_send()
+
+    second_norm(0)
+    second_norm(1)
+    feed_up(0)
+    second_norm(2)
+    feed_up(1)
+    feed_up(2)
     rs_first(3)
+    ag_wait(3)
+    feed_back(0)
+    feed_back(1)
+    ps_mid(1, 0)
+    feed_back(2)
+    ps_mid(1, 1)
+    g.ntT[...] = jnp.transpose(g.ntk[...])
     ps_mid(1, 2)
-    g.ntT[...] = jnp.transpose(g.ntk[...])
-    rs_first(2)
 
     def add_sum(row, value):
         g.sums[row : row + 1, :] += jnp.sum(value, axis=0, keepdims=True)
@@ -752,24 +828,23 @@
 
     def grad_attended(r):
         share_wait(g.gb, r, g.gb_s, g.gb_r)
-        ga = jnp.transpose(nn(g.gb[rows(r), :], g.wo[...].reshape(768, 192))).astype(BF)
+        ga = jnp.transpose(nn(g.gb[rows(r), :], g.wo[...])).astype(BF)
         for i in range(4):
             g.snD[i, r] = ga[48 * i : 48 * i + 48]
             send_part(i, r, g.snD, g.rcD, g.d_s, g.d_r)
 
     second_back(0)
+    rs_second(3, 0)
     second_back(1)
     grad_attended(0)
     second_back(2)
     grad_attended(1)
     grad_attended(2)
-
+    rs_second(3, 1)
+    rs_first(2, 0, 2)
     for r in range(R):
         ps_start(2, r, nt(g.act[rows(r), :], g.wd[...].reshape(768, 768)))
     g.gbT[...] = jnp.transpose(g.gb[...])
-    rs_first(1)
-    for r in range(R):
-        ps_mid(2, r)
 
     def attn_bwd(r):
         for i in range(4):
@@ -806,14 +881,21 @@
             send_part(i, r, g.snG, g.rcG, g.g_s, g.g_r)
 
     attn_bwd(0)
-    rs_second(3)
+    ps_mid(2, 0)
+    attn_bwd(1)
     attn_bwd_end(0)
-    attn_bwd(1)
-    rs_second(2)
+    rs_first(2, 2, 3)
+    ps_mid(2, 1)
+    attn_bwd(2)
     attn_bwd_end(1)
-    attn_bwd(2)
-    rs_second(1)
+    rs_first(2, 3, 4)
+    ps_mid(2, 2)
     attn_bwd_end(2)
+    rs_second(3, 2)
+    rs_first(1)
+    rs_second(2, 0)
+    rs_second(2, 1)
+    rs_own(3)
 
     for r in range(R):
         g.out_tok[half(r, c), :] = (g.mid[r] + ps_end(2, r) + ob1).astype(BF)
@@ -821,23 +903,28 @@
     ones = jnp.ones((8, 384), BF)
     g.sums[6:7, :] = nn(ones, g.gp[...])[0:1]
 
-    for r in range(R):
+    def project_back(r):
         for i in range(4):
             wait_part(i, r, g.rcG, g.g_s, g.g_r)
             for t in range(3):
                 g.gpT[192 * t + 48 * i : 192 * t + 48 * i + 48, 128 * r : 128 * r + 128] = g.rcG[
                     i, r, 48 * t : 48 * t + 48, :
                 ]
-        ps_start(3, r, tt(g.gpT[:, 128 * r : 128 * r + 128], g.wq[:, 0:96, :].reshape(768, 576)))
-        if r > 0:
-            ps_mid(3, r - 1)
+        ps_start(3, r, tt(g.gpT[:, 128 * r : 128 * r + 128], g.wq[:, :, 0:576].reshape(768, 576)))
+
+    project_back(0)
+    rs_second(2, 2)
+    project_back(1)
+    ps_mid(3, 0)
+    rs_own(2)
+    project_back(2)
+    ps_mid(3, 1)
     rs_first(0)
-    ps_mid(3, R - 1)
+    ps_mid(3, 2)
+    for t in range(3):
+        rs_second(1, t)
+    rs_own(1)
     g.sums[7:8, 0:576] = nt(ones, g.gpT[...])[0:1]
-
-    rs_third(3)
-    rs_third(2)
-    rs_third(1)
 
     def first_back(r):
         gn = ps_end(3, r)
@@ -851,30 +938,45 @@
     for r in range(R):
         first_back(r)
     rdma(g.sums, g.sumA, g.sm_s.at[0], g.sm_r.at[0], sib).start()
-    rs_second(0)
     rdma(g.sumA, g.sumA, g.sm_s.at[0], g.sm_r.at[0], sib).wait_recv()
     both = lax.broadcasted_iota(jnp.int32, (8, 768), 0) < 6
     g.sumB[...] = g.sums[...] + jnp.where(both, g.sumA[...], 0.0)
     rdma(g.sumB, g.sumC, g.sm_s.at[1], g.sm_r.at[1], yp).start()
+    for t in range(3):
+        rs_second(0, t)
     rdma(g.sumC, g.sumC, g.sm_s.at[1], g.sm_r.at[1], yp).wait_recv()
     g.sumD[z] = g.sumB[...] + g.sumC[...]
     for t in range(3):
         rdma(g.sumD.at[z], g.sumD.at[z], g.sm_s.at[2 + t], g.sm_r.at[2 + z], zm[t]).start()
-    rs_third(0)
+    rs_own(0)
+    rs_third(3)
+    rs_third(2)
+    g.out_gout[...] = jnp.transpose(rs_third(1))
+    total = rs_third(0)
+    for t in range(3):
+        g.out_gqkv[t] = total[:, 192 * t : 192 * t + 192]
     for t in range(3):
         q = zs[t]
         rdma(g.sumD.at[q], g.sumD.at[q], g.sm_s.at[2 + t], g.sm_r.at[2 + q], zm[t]).wait_recv()
     total = g.sumD[0] + g.sumD[1] + g.sumD[2] + g.sumD[3]
-    g.out_sums[...] = total
     for k in range(8):
         g.cut[k] = total[:, 96 * k : 96 * k + 96]
-    g.out_cut[...] = g.cut[s]
+    mine = g.cut[s]
+    g.out_gain[...] = mine[0:2]
+    g.out_shift[...] = mine[2:4]
+    g.out_obias[...] = mine[4:6]
+    g.out_upb[...] = total[6:7]
+    g.out_qvb[0:1, :] = total[7:8, 0:192]
+    g.out_qvb[1:2, :] = total[7:8, 384:576]
 
     for r in range(R):
         share_wait(g.out_tok, r, g.ot_s, g.ot_r)
         share_wait(g.out_gtok, r, g.gt_s, g.gt_r)
+    for t, dev in enumerate(others):
+        rdma(g.sml.at[s], g.sml.at[s], g.sml_s.at[t], g.sml_r.at[s], dev).wait_send()
+    for p in (0, 2, 3):
+        ag_drain(p)
     for p in range(4):
-        ag_drain(p)
         rs_drain(p)
     for r in range(R):
         for i in range(4):
@@ -887,7 +989,7 @@
         for kind in range(4):
             for t in range(2):
                 rdma(
-                    g.psH.at[kind, r], g.psB.at[kind, r], g.ps_s.at[kind, r, t], g.ps_r.at[kind, r, t], xp
+                    g.psH.at[kind, r], g.psB.at[kind, r], PSS[kind].at[r, t], PSR[kind].at[r, t], xp
                 ).wait_send()
         for ref, ss, rs in (
             (g.ntk, g.nt_s, g.nt_r),
@@ -906,36 +1008,44 @@
     tokens, cotangent, lengths, coords, keep_mask, ln_gains, ln_shifts, out_bias,
     w_qkv, qv_bias, w_out, w_up, up_bias, w_down,
 ):
-    small = jnp.concatenate([ln_gains, ln_shifts, out_bias], axis=0)
-    small = jnp.pad(small, ((0, 0), (0, 480)))
-    keep = jnp.pad(keep_mask.astype(BF), ((0, 7), (0, 448)))
-    shard = jnp.concatenate([w_qkv.reshape(96, 576), small, keep], axis=0)
-    crd = jnp.pad(jnp.transpose(coords, (1, 0, 2)).astype(F32), ((0, 0), (0, 6), (0, 0)))
     inputs = [
         ("in_tok", tokens.reshape(384, 768)),
         ("in_cot", cotangent.reshape(384, 768)),
         ("in_len", lengths),
-        ("in_crd", crd),
-        ("in_wq", shard),
+        ("in_crd", jnp.transpose(coords, (1, 0, 2))),
+        ("in_keep", keep_mask),
+        ("in_lng", ln_gains),
+        ("in_lns", ln_shifts),
+        ("in_ob", out_bias),
+        ("in_w3", jnp.transpose(w_qkv, (1, 0, 2))),
         ("in_qvb", qv_bias),
         ("in_wo", w_out),
         ("in_wu", w_up),
         ("in_upb", up_bias.reshape(1, 768)),
-        ("in_wd", w_down),
+        ("in_wd", jnp.transpose(w_down)),
     ]
     outputs = [
         ("out_tok", (384, 768), BF),
         ("out_gtok", (384, 768), BF),
-        ("out_gqkv", (96, 576), F32),
-        ("out_gout", (96, 192), F32),
+        ("out_gain", (2, 96), F32),
+        ("out_shift", (2, 96), F32),
+        ("out_obias", (2, 96), F32),
+        ("out_gqkv", (3, 96, 192), F32),
+        ("out_qvb", (2, 192), F32),
+        ("out_gout", (192, 96), F32),
         ("out_gup", (96, 768), F32),
+        ("out_upb", (1, 768), F32),
         ("out_gdown", (96, 768), F32),
-        ("out_sums", (8, 768), F32),
-        ("out_cut", (8, 96), F32),
     ]
     vm = [
-        ("wq", (8, 112, 576), BF),
-        ("wo", (8, 96, 192), BF),
+        ("wq", (8, 96, 768), BF),
+        ("wo", (768, 192), BF),
+        ("sml", (8, 16, 128), BF),
+        ("tmp", (16, 128), F32),
+        ("nrm", (384, 768), BF),
+        ("gd", (384, 768), F32),
+        ("acc0", (96, 576), F32),
+        ("acc1", (96, 192), F32),
         ("wu", (8, 96, 768), BF),
         ("wd", (8, 96, 768), BF),
         ("inp", (384, 768), F32),
@@ -989,22 +1099,24 @@
         for kind in ("l1s", "l1r", "l2s", "l2r"):
             vm.append((f"{kind}{p}", (4, 96, width), BF))
     sems = [
-        ("ag_s", (4, 7)), ("ag_r", (4, 8)),
         ("qa_s", (4, 3)), ("qa_r", (4, 3)),
         ("sa_s", (4, 3)), ("sa_r", (4, 3)),
         ("o_s", (4, 3)), ("o_r", (4, 3)),
         ("d_s", (4, 3)), ("d_r", (4, 3)),
         ("g_s", (4, 3)), ("g_r", (4, 3)),
         ("x_s", (3,)), ("x_r", (3,)),
-        ("ps_s", (4, 3, 2)), ("ps_r", (4, 3, 2)),
         ("nt_s", (3,)), ("nt_r", (3,)),
         ("gb_s", (3,)), ("gb_r", (3,)),
         ("ot_s", (3,)), ("ot_r", (3,)),
         ("gt_s", (3,)), ("gt_r", (3,)),
-        ("l1_s", (4, 4)), ("l1_r", (4, 4)),
-        ("l2_s", (4, 4)), ("l2_r", (4, 4)),
         ("sm_s", (8,)), ("sm_r", (8,)),
+        ("sml_s", (7,)), ("sml_r", (8,)),
     ]
+    for name, shape in (
+        ("ag_s", (8,)), ("ag_r", (8,)), ("ps_s", (3, 2)), ("ps_r", (3, 2)),
+        ("l1_s", (4,)), ("l1_r", (4,)), ("l2_s", (4,)), ("l2_r", (4,)),
+    ):
+        sems += [(f"{name}{q}", shape) for q in range(4)]
     names = [n for n, _ in inputs] + [o[0] for o in outputs] + [v[0] for v in vm] + [n for n, _ in sems]
     vmem = pl.BlockSpec(memory_space=pltpu.VMEM)
     out = pl.pallas_call(
@@ -1020,18 +1132,30 @@
             collective_id=0, has_side_effects=True, vmem_limit_bytes=60 * 1024 * 1024
         ),
     )(*[v for _, v in inputs])
-    out_tok, out_gtok, gqkv, gout, gup, gdown, sums, cut = out
+    shapes = [jax.ShapeDtypeStruct(o.shape, o.dtype) for o in out]
+
+    def hand_over(*refs):
+        for n in range(len(shapes)):
+            refs[len(shapes) + n][...] = refs[n][...]
+
+    out = pl.pallas_call(
+        hand_over,
+        out_shape=shapes,
+        in_specs=[vmem] * len(shapes),
+        out_specs=[vmem] * len(shapes),
+    )(*out)
+    out_tok, out_gtok, gain, shift, obias, gqkv, qvb, gout, gup, upb, gdown = out
     return (
         out_tok.reshape(3, 128, 768),
         out_gtok.reshape(3, 128, 768),
-        cut[0:2],
-        cut[2:4],
-        cut[4:6],
-        gqkv.reshape(96, 3, 192),
-        jnp.stack([sums[7, 0:192], sums[7, 384:576]]),
-        jnp.transpose(gout),
+        gain,
+        shift,
+        obias,
+        jnp.transpose(gqkv, (1, 0, 2)),
+        qvb,
+        gout,
         gup,
-        sums[6],
+        upb.reshape(768),
         jnp.transpose(gdown),
     )
 

time: 189 us -> 136 us (0.72)
  Pallas kernels: 171 us -> 132 us
  local copies, waits for them, and re-layouts: 15.3 us -> 1.94 us
    pallas_call x1, Pallas kernels: 171 us -> 129 us  [fast_device(): pl.pallas_call(partial(layer_kernel, names=names), out_shape=[jax.ShapeDt...]
    unnamed x32 -> x4, local copies, waits for them, and re-layouts: 10.3 us -> 1.36 us
    slice x3 -> x0, local copies, waits for them, and re-layouts: 3.47 us -> none  [the longest x1 1.36 us: fast_device(): cut[4:6]]
    pallas_call x0 -> x1, Pallas kernels: none -> 2.95 us  [fast_device(): pl.pallas_call(hand_over, out_shape=shapes, in_specs=[vmem] * len(shapes)...]
where the time goes in v2:
time: 136 us
  Pallas kernels  132 us (97%)
  local copies, waits for them, and re-layouts  1.94 us (1%)
    pallas_call x1, Pallas kernels, fast_device(): pl.pallas_call(partial(layer_kernel, names=names), out_shape=[jax.ShapeDt...  129 us
    pallas_call x1, Pallas kernels, fast_device(): pl.pallas_call(hand_over, out_shape=shapes, in_specs=[vmem] * len(shapes)...  2.95 us

profile of v2, /device:TPU:0, one launch (start us, length us, event | category | flops | bytes accessed | tf_op | source)
XLA Modules:
  0.0 135.6 jit_solution(18401110706555914395)
XLA Ops:
  0.6 0.0 copy-start.1
  0.7 0.7 copy-done.1
  1.3 0.6 reshape.42.refs_12_
  1.9 129.4 %shard_map.221 = (bf16[384,768]{1,0:T(8,128)(2,1)}, bf16[384,768]{1,0:T(8,128)(2,1)}, f32[2,96]{1,0:T(2,128)}, f32[2,96]{1,0:T(2,128)}, f32[2,96]{1,0:T(2,128)},...) custom-call(bf16[384,768]{1,0:T(8,128)(2,1)} %bitcast.9, ...), custom_call_target="tpu_custom_call" | custom-call | tf_op jit(solution)/shard_map/pallas_call | solution.py:1122
  131.3 3.0 %shard_map.222 = (bf16[384,768]{1,0:T(8,128)(2,1)}, bf16[384,768]{1,0:T(8,128)(2,1)}, f32[2,96]{1,0:T(2,128)}, f32[2,96]{1,0:T(2,128)}, f32[2,96]{1,0:T(2,128)},...) custom-call(bf16[384,768]{1,0:T(8,128)(2,1)} %get-tuple-element.33.r, ...), custom_call_target="tpu_custom_call" | custom-call | tf_op jit(solution)/shard_map/pallas_call | solution.py:1141
  134.3 0.0 copy-start
  134.3 0.7 copy-done
  135.0 0.6 reduce
Async XLA Ops:
  0.6 0.7 copy-start.1
  134.3 0.7 copy-start

commit v3 on v2

--- a/solution.py
+++ b/solution.py
@@ -427,7 +427,10 @@
         def _():
             pl.semaphore_signal(bar, inc=1, device_id=part[i], device_id_type=MESH)
 
-    W = [g.wq, None, g.wu, g.wd]
+    def piece(p, k):
+        if p < 2:
+            return g.wq.at[k, pl.ds(48 * p, 48)]
+        return (g.wu if p == 2 else g.wd).at[k]
 
     def four_of(name):
         return [r_[f"{name}{q}"] for q in range(4)]
@@ -436,45 +439,45 @@
     L1SS, L1RS, L2SS, L2RS = four_of("l1_s"), four_of("l1_r"), four_of("l2_s"), four_of("l2_r")
 
     def ag_y(p):
-        w = W[p]
-        rdma(w.at[s], w.at[s], AGS[p].at[0], AGR[p].at[s], yp).start()
+        rdma(piece(p, s), piece(p, s), AGS[p].at[0], AGR[p].at[s], yp).start()
 
     def ag_z(p):
-        w = W[p]
-        for t in range(2):
-            rdma(w.at[s], w.at[s], AGS[p].at[1 + t], AGR[p].at[s], zm[t]).start()
+        @pl.when(outer)
+        def _():
+            for t in (1, 0):
+                rdma(piece(p, s), piece(p, s), AGS[p].at[1 + t], AGR[p].at[s], zm[t]).start()
 
         @pl.when(inner)
         def _():
-            rdma(w.at[s], w.at[s], AGS[p].at[3], AGR[p].at[s], zm[2]).start()
+            for t in range(3):
+                rdma(piece(p, s), piece(p, s), AGS[p].at[1 + t], AGR[p].at[s], zm[t]).start()
 
     def ag_forward(p, t):
-        w = W[p]
         k = zm[t][0]
-        rdma(w.at[k], w.at[k], AGS[p].at[4 + t], AGR[p].at[k], zm[t]).wait_recv()
+        w = piece(p, k)
+        rdma(w, w, AGS[p].at[4 + t], AGR[p].at[k], zm[t]).wait_recv()
         if t == 2:
 
             @pl.when(inner)
             def _():
-                rdma(w.at[k], w.at[k], AGS[p].at[7], AGR[p].at[k], zm[0]).start()
-
-        rdma(w.at[k], w.at[k], AGS[p].at[4 + t], AGR[p].at[k], yp).start()
+                rdma(w, w, AGS[p].at[7], AGR[p].at[k], zm[0]).start()
+
+        rdma(w, w, AGS[p].at[4 + t], AGR[p].at[k], yp).start()
 
     def ag_wait(p):
-        w = W[p]
         for q in qs:
-            k = 2 * q + 1 - y
-            rdma(w.at[k], w.at[k], AGS[p].at[0], AGR[p].at[k], yp).wait_recv()
+            w = piece(p, 2 * q + 1 - y)
+            rdma(w, w, AGS[p].at[0], AGR[p].at[2 * q + 1 - y], yp).wait_recv()
 
     def ag_drain(p):
-        w = W[p]
+        w = piece(p, s)
         for t in (0, 1, 2, 4, 5, 6):
-            rdma(w.at[s], w.at[s], AGS[p].at[t], AGR[p].at[s], yp).wait_send()
+            rdma(w, w, AGS[p].at[t], AGR[p].at[s], yp).wait_send()
 
         @pl.when(inner)
         def _():
             for t in (3, 7):
-                rdma(w.at[s], w.at[s], AGS[p].at[t], AGR[p].at[s], yp).wait_send()
+                rdma(w, w, AGS[p].at[t], AGR[p].at[s], yp).wait_send()
 
     g.wq[s] = jnp.concatenate(
         [g.in_w3[0], g.in_w3[1], g.in_w3[2], jnp.transpose(g.in_wo[...])], axis=1
@@ -491,10 +494,12 @@
     others = [yp] + zm + zy
     for t, dev in enumerate(others):
         rdma(g.sml.at[s], g.sml.at[s], g.sml_s.at[t], g.sml_r.at[s], dev).start()
-    ag_y(0)
-    ag_z(0)
+    for p in range(2):
+        ag_y(p)
+        ag_z(p)
     ag_y(2)
     ag_z(2)
+    ag_y(3)
 
     lane = lax.broadcasted_iota(jnp.int32, (1, 768), 1)
     freq = jnp.exp(
@@ -537,9 +542,15 @@
         nr = (g.n1[rows(r), :] * g0 + par[2:3]).astype(BF)
         g.nrm[rows(r), :] = nr
         g.nrmT[:, 128 * r : 128 * r + 128] = jnp.transpose(nr)
-    for t in range(3):
-        ag_forward(0, t)
+    ag_forward(0, 0)
+    ag_forward(1, 0)
+    ag_forward(0, 1)
+    ag_forward(1, 1)
+    ag_forward(0, 2)
+    ag_forward(1, 2)
+    ag_forward(2, 0)
     ag_wait(0)
+    ag_wait(1)
 
     def send_part(i, r, src, dst, ss, rs):
         @pl.when(not_own(i))
@@ -567,11 +578,10 @@
             for t in range(3):
                 g.snA[i, r, 48 * t : 48 * t + 48, :] = projT[192 * t + 48 * i : 192 * t + 48 * i + 48]
             send_part(i, r, g.snA, g.rcA, g.qa_s, g.qa_r)
-
-    ag_y(3)
-    for t in range(3):
-        ag_forward(2, t)
+        if r == 1:
+            ag_forward(2, 1)
     ag_z(3)
+
     g.wo[...] = g.wq[:, :, 576:768].reshape(768, 192)
 
     def slide_of_row(r, pos):
@@ -636,9 +646,10 @@
                 send_part(i, r, g.snO, g.rcO, g.o_s, g.o_r)
 
     attn_fwd(0)
+    ag_forward(2, 2)
     attn_fwd(1)
+    ag_forward(3, 0)
     attn_fwd(2)
-    ag_forward(3, 0)
 
     def ps_start(kind, r, part_sum):
         g.ps[kind, r] = part_sum.astype(BF)
@@ -679,7 +690,8 @@
         ps_start(0, r, nt(att, g.wo[...]))
         if r > 0:
             ps_mid(0, r - 1)
-    ag_forward(3, 1)
+        if r == 1:
+            ag_forward(3, 1)
     ps_mid(0, R - 1)
     ag_forward(3, 2)
     ag_wait(2)
@@ -695,7 +707,7 @@
         g.ntk[half(r, c), :] = (v * g1 + s1).astype(BF)
         share_start(g.ntk, r, g.nt_s, g.nt_r)
 
-    up_bias = g.in_upb[...].astype(F32)
+    up_bias = g.in_upb[...].astype(F32).reshape(1, 768)
 
     def feed_up(r):
         share_wait(g.ntk, r, g.nt_s, g.nt_r)
@@ -710,7 +722,26 @@
         g.gp[rows(r), :] = (gact * g.gd[rows(r), :]).astype(BF)
         ps_start(1, r, nt(g.gp[rows(r), :], g.wu[...].reshape(768, 768)))
 
+    def pack(v):
+        width = v.shape[1]
+        tiles = [v[:, 128 * t : 128 * t + 128] for t in range(width // 128)]
+        if width % 128:
+            rest = v[:, width - 64 :]
+            tiles.append(jnp.concatenate([rest[0:48], rest[48:96]], axis=1))
+        return jnp.concatenate(tiles, axis=0)
+
+    def unpack(v):
+        count = v.shape[0] // 96
+        tiles = [v[96 * t : 96 * t + 96] for t in range(count)]
+        if v.shape[0] % 96:
+            rest = v[96 * count :]
+            tiles.append(jnp.concatenate([rest[:, 0:64], rest[:, 64:128]], axis=0))
+        return jnp.concatenate(tiles, axis=1)
+
     def block(p, k):
+        return pack(raw_block(p, k))
+
+    def raw_block(p, k):
         b = pl.ds(pl.multiple_of(96 * k, 96), 96)
         if p == 0:
             return nt(g.nrmT[b, :], g.gpT[...])
@@ -724,42 +755,45 @@
     L1R = [g.l1r0, g.l1r1, g.l1r2, g.l1r3]
     L2S = [g.l2s0, g.l2s1, g.l2s2, g.l2s3]
     L2R = [g.l2r0, g.l2r1, g.l2r2, g.l2r3]
-    g.acc = [g.acc0, g.acc1, g.out_gup, g.out_gdown]
+    g.acc = [g.acc0, g.acc1, g.acc2, g.acc3]
 
     def rs_first(p, start=0, stop=4):
         def step(t, _):
-            q = four(t, qs)
+            q = four(t, [zs[2], zs[1], zs[0], z])
             L1S[p][q] = block(p, 2 * q + 1 - y).astype(BF)
             rdma(L1S[p].at[q], L1R[p].at[q], L1SS[p].at[q], L1RS[p].at[q], yp).start()
             return 0
 
         lax.fori_loop(start, stop, step, 0)
 
+    def reduced(p, q):
+        dst = L1R[p].at[q]
+        rdma(dst, dst, L1SS[p].at[q], L1RS[p].at[q], yp).wait_recv()
+        return block(p, 2 * q + y) + L1R[p][q].astype(F32)
+
+    def rs_far(p):
+        @pl.when(outer)
+        def _():
+            q = zs[2]
+            L2S[p][q] = reduced(p, q).astype(BF)
+            rdma(L2S[p].at[q], L2R[p].at[zs[0]], L2SS[p].at[q], L2RS[p].at[zs[0]], zm[0]).start()
+
     def rs_second(p, t):
         q = zs[t]
-        dst = L1R[p].at[q]
-        rdma(dst, dst, L1SS[p].at[q], L1RS[p].at[q], yp).wait_recv()
-        mine = block(p, 2 * q + y) + L1R[p][q].astype(F32)
 
         def send():
+            v = reduced(p, q)
+            if t == 2:
+                via = L2R[p].at[z]
+                rdma(via, via, L2SS[p].at[q], L2RS[p].at[z], zm[0]).wait_recv()
+                v = v + via[...].astype(F32)
+            L2S[p][q] = v.astype(BF)
             rdma(L2S[p].at[q], L2R[p].at[z], L2SS[p].at[q], L2RS[p].at[z], zm[t]).start()
 
-        if t < 2:
-            L2S[p][q] = mine.astype(BF)
+        if t == 2:
+            pl.when(inner)(send)
+        else:
             send()
-        else:
-            via = L2R[p].at[z]
-
-            @pl.when(outer)
-            def _():
-                L2S[p][q] = mine.astype(BF)
-                rdma(L2S[p].at[q], L2R[p].at[zs[0]], L2SS[p].at[q], L2RS[p].at[zs[0]], zm[0]).start()
-
-            @pl.when(inner)
-            def _():
-                rdma(via, via, L2SS[p].at[q], L2RS[p].at[z], zm[0]).wait_recv()
-                L2S[p][q] = (mine + via[...].astype(F32)).astype(BF)
-                send()
 
     def rs_own(p):
         dst = L1R[p].at[z]
@@ -779,7 +813,7 @@
                 add()
             else:
                 pl.when(inner)(add)
-        return acc[...]
+        return unpack(acc[...])
 
     def rs_drain(p):
         for q in qs:
@@ -793,15 +827,18 @@
     second_norm(2)
     feed_up(1)
     feed_up(2)
-    rs_first(3)
+    rs_first(3, 0, 1)
     ag_wait(3)
     feed_back(0)
     feed_back(1)
     ps_mid(1, 0)
+    rs_first(3, 1, 2)
     feed_back(2)
     ps_mid(1, 1)
+    rs_first(3, 2, 3)
+    ps_mid(1, 2)
+    rs_first(3, 3, 4)
     g.ntT[...] = jnp.transpose(g.ntk[...])
-    ps_mid(1, 2)
 
     def add_sum(row, value):
         g.sums[row : row + 1, :] += jnp.sum(value, axis=0, keepdims=True)
@@ -834,7 +871,7 @@
             send_part(i, r, g.snD, g.rcD, g.d_s, g.d_r)
 
     second_back(0)
-    rs_second(3, 0)
+    rs_far(3)
     second_back(1)
     grad_attended(0)
     second_back(2)
@@ -891,9 +928,10 @@
     rs_first(2, 3, 4)
     ps_mid(2, 2)
     attn_bwd_end(2)
+    rs_second(3, 0)
     rs_second(3, 2)
     rs_first(1)
-    rs_second(2, 0)
+    rs_far(2)
     rs_second(2, 1)
     rs_own(3)
 
@@ -913,17 +951,21 @@
         ps_start(3, r, tt(g.gpT[:, 128 * r : 128 * r + 128], g.wq[:, :, 0:576].reshape(768, 576)))
 
     project_back(0)
-    rs_second(2, 2)
+    rs_second(2, 0)
     project_back(1)
     ps_mid(3, 0)
-    rs_own(2)
+    rs_second(2, 2)
     project_back(2)
     ps_mid(3, 1)
-    rs_first(0)
+    rs_first(0, 0, 2)
     ps_mid(3, 2)
-    for t in range(3):
+    rs_first(0, 2, 4)
+    rs_own(2)
+    rs_far(1)
+    for t in (1, 0, 2):
         rs_second(1, t)
     rs_own(1)
+    rs_far(0)
     g.sums[7:8, 0:576] = nt(ones, g.gpT[...])[0:1]
 
     def first_back(r):
@@ -942,15 +984,15 @@
     both = lax.broadcasted_iota(jnp.int32, (8, 768), 0) < 6
     g.sumB[...] = g.sums[...] + jnp.where(both, g.sumA[...], 0.0)
     rdma(g.sumB, g.sumC, g.sm_s.at[1], g.sm_r.at[1], yp).start()
-    for t in range(3):
+    for t in (1, 0, 2):
         rs_second(0, t)
     rdma(g.sumC, g.sumC, g.sm_s.at[1], g.sm_r.at[1], yp).wait_recv()
     g.sumD[z] = g.sumB[...] + g.sumC[...]
     for t in range(3):
         rdma(g.sumD.at[z], g.sumD.at[z], g.sm_s.at[2 + t], g.sm_r.at[2 + z], zm[t]).start()
     rs_own(0)
-    rs_third(3)
-    rs_third(2)
+    g.out_gdown[...] = rs_third(3)
+    g.out_gup[...] = rs_third(2)
     g.out_gout[...] = jnp.transpose(rs_third(1))
     total = rs_third(0)
     for t in range(3):
@@ -974,7 +1016,7 @@
         share_wait(g.out_gtok, r, g.gt_s, g.gt_r)
     for t, dev in enumerate(others):
         rdma(g.sml.at[s], g.sml.at[s], g.sml_s.at[t], g.sml_r.at[s], dev).wait_send()
-    for p in (0, 2, 3):
+    for p in range(4):
         ag_drain(p)
     for p in range(4):
         rs_drain(p)
@@ -1021,7 +1063,7 @@
         ("in_qvb", qv_bias),
         ("in_wo", w_out),
         ("in_wu", w_up),
-        ("in_upb", up_bias.reshape(1, 768)),
+        ("in_upb", up_bias),
         ("in_wd", jnp.transpose(w_down)),
     ]
     outputs = [
@@ -1044,8 +1086,10 @@
         ("tmp", (16, 128), F32),
         ("nrm", (384, 768), BF),
         ("gd", (384, 768), F32),
-        ("acc0", (96, 576), F32),
-        ("acc1", (96, 192), F32),
+        ("acc0", (432, 128), F32),
+        ("acc1", (144, 128), F32),
+        ("acc2", (576, 128), F32),
+        ("acc3", (576, 128), F32),
         ("wu", (8, 96, 768), BF),
         ("wd", (8, 96, 768), BF),
         ("inp", (384, 768), F32),
@@ -1097,7 +1141,7 @@
     ]
     for p, width in enumerate((576, 192, 768, 768)):
         for kind in ("l1s", "l1r", "l2s", "l2r"):
-            vm.append((f"{kind}{p}", (4, 96, width), BF))
+            vm.append((f"{kind}{p}", (4, 96 * width // 128, 128), BF))
     sems = [
         ("qa_s", (4, 3)), ("qa_r", (4, 3)),
         ("sa_s", (4, 3)), ("sa_r", (4, 3)),
@@ -1132,11 +1176,13 @@
             collective_id=0, has_side_effects=True, vmem_limit_bytes=60 * 1024 * 1024
         ),
     )(*[v for _, v in inputs])
-    shapes = [jax.ShapeDtypeStruct(o.shape, o.dtype) for o in out]
+    shapes = [
+        jax.ShapeDtypeStruct((768,) if o.shape == (1, 768) else o.shape, o.dtype) for o in out
+    ]
 
     def hand_over(*refs):
         for n in range(len(shapes)):
-            refs[len(shapes) + n][...] = refs[n][...]
+            refs[len(shapes) + n][...] = refs[n][...].reshape(shapes[n].shape)
 
     out = pl.pallas_call(
         hand_over,
@@ -1155,7 +1201,7 @@
         qvb,
         gout,
         gup,
-        upb.reshape(768),
+        upb,
         jnp.transpose(gdown),
     )
 

time: 136 us -> 129 us (0.949)
  Pallas kernels: 132 us -> 128 us
  local copies, waits for them, and re-layouts: 1.94 us -> 0 us
    pallas_call x1, Pallas kernels: 129 us -> 125 us  [fast_device(): pl.pallas_call(partial(layer_kernel, names=names), out_shape=[jax.ShapeDt...]
where the time goes in v3:
time: 129 us
  Pallas kernels  128 us (99%)
    pallas_call x1, Pallas kernels, fast_device(): pl.pallas_call(partial(layer_kernel, names=names), out_shape=[jax.ShapeDt...  125 us
    pallas_call x1, Pallas kernels, fast_device(): pl.pallas_call(hand_over, out_shape=shapes, in_specs=[vmem] * len(shapes)...  2.95 us

profile of v3, /device:TPU:0, one launch (start us, length us, event | category | flops | bytes accessed | tf_op | source)
XLA Modules:
  0.0 128.9 jit_solution(8851239950555040981)
XLA Ops:
  0.6 125.3 %shard_map.221 = (bf16[384,768]{1,0:T(8,128)(2,1)}, bf16[384,768]{1,0:T(8,128)(2,1)}, f32[2,96]{1,0:T(2,128)}, f32[2,96]{1,0:T(2,128)}, f32[2,96]{1,0:T(2,128)},...) custom-call(bf16[384,768]{1,0:T(8,128)(2,1)} %bitcast.9, ...), custom_call_target="tpu_custom_call" | custom-call | tf_op jit(solution)/shard_map/pallas_call | solution.py:1166
  125.9 3.0 %shard_map.222 = (bf16[384,768]{1,0:T(8,128)(2,1)}, bf16[384,768]{1,0:T(8,128)(2,1)}, f32[2,96]{1,0:T(2,128)}, f32[2,96]{1,0:T(2,128)}, f32[2,96]{1,0:T(2,128)},...) custom-call(bf16[384,768]{1,0:T(8,128)(2,1)} %get-tuple-element.33.r, ...), custom_call_target="tpu_custom_call" | custom-call | tf_op jit(solution)/shard_map/pallas_call | solution.py:1187

commit v4 on v3

--- a/solution.py
+++ b/solution.py
@@ -948,6 +948,8 @@
                 g.gpT[192 * t + 48 * i : 192 * t + 48 * i + 48, 128 * r : 128 * r + 128] = g.rcG[
                     i, r, 48 * t : 48 * t + 48, :
                 ]
+        if r == R - 1:
+            rs_first(0, 0, 2)
         ps_start(3, r, tt(g.gpT[:, 128 * r : 128 * r + 128], g.wq[:, :, 0:576].reshape(768, 576)))
 
     project_back(0)
@@ -957,9 +959,8 @@
     rs_second(2, 2)
     project_back(2)
     ps_mid(3, 1)
-    rs_first(0, 0, 2)
+    rs_first(0, 2, 4)
     ps_mid(3, 2)
-    rs_first(0, 2, 4)
     rs_own(2)
     rs_far(1)
     for t in (1, 0, 2):
@@ -977,15 +978,17 @@
         add_sum(0, gn * n)
         add_sum(2, gn)
 
-    for r in range(R):
-        first_back(r)
+    first_back(0)
+    first_back(1)
+    rs_second(0, 1)
+    first_back(2)
     rdma(g.sums, g.sumA, g.sm_s.at[0], g.sm_r.at[0], sib).start()
     rdma(g.sumA, g.sumA, g.sm_s.at[0], g.sm_r.at[0], sib).wait_recv()
     both = lax.broadcasted_iota(jnp.int32, (8, 768), 0) < 6
     g.sumB[...] = g.sums[...] + jnp.where(both, g.sumA[...], 0.0)
     rdma(g.sumB, g.sumC, g.sm_s.at[1], g.sm_r.at[1], yp).start()
-    for t in (1, 0, 2):
-        rs_second(0, t)
+    rs_second(0, 0)
+    rs_second(0, 2)
     rdma(g.sumC, g.sumC, g.sm_s.at[1], g.sm_r.at[1], yp).wait_recv()
     g.sumD[z] = g.sumB[...] + g.sumC[...]
     for t in range(3):

time: 129 us -> 129 us (level)
  no operation moved by 1% of the time
where the time goes in v4:
time: 129 us; the launch traced here: 128 us
  Pallas kernels  128 us (99%)
    pallas_call x1, Pallas kernels, fast_device(): pl.pallas_call(partial(layer_kernel, names=names), out_shape=[jax.ShapeDt...  125 us
    pallas_call x1, Pallas kernels, fast_device(): pl.pallas_call(hand_over, out_shape=shapes, in_specs=[vmem] * len(shapes)...  2.95 us

profile of v4, /device:TPU:0, one launch (start us, length us, event | category | flops | bytes accessed | tf_op | source)
XLA Modules:
  0.0 128.4 jit_solution(16280405644246391780)
XLA Ops:
  0.6 124.8 %shard_map.221 = (bf16[384,768]{1,0:T(8,128)(2,1)}, bf16[384,768]{1,0:T(8,128)(2,1)}, f32[2,96]{1,0:T(2,128)}, f32[2,96]{1,0:T(2,128)}, f32[2,96]{1,0:T(2,128)},...) custom-call(bf16[384,768]{1,0:T(8,128)(2,1)} %bitcast.9, ...), custom_call_target="tpu_custom_call" | custom-call | tf_op jit(solution)/shard_map/pallas_call | solution.py:1169
  125.4 3.0 %shard_map.222 = (bf16[384,768]{1,0:T(8,128)(2,1)}, bf16[384,768]{1,0:T(8,128)(2,1)}, f32[2,96]{1,0:T(2,128)}, f32[2,96]{1,0:T(2,128)}, f32[2,96]{1,0:T(2,128)},...) custom-call(bf16[384,768]{1,0:T(8,128)(2,1)} %get-tuple-element.33.r, ...), custom_call_target="tpu_custom_call" | custom-call | tf_op jit(solution)/shard_map/pallas_call | solution.py:1190
